TPU v7x, 128 devices: a whole 4x4x4 slice. The times are simulated.
128 devices in a mesh: dp: 16 (over x, y_lo, core), sample: 8 (over y_hi, z).
Axes of the slice: x: 4, y: 4 (y_hi: 2, y_lo: 2; y = y_hi * 2 + y_lo), z: 4, core: 2. Of those that a mesh axis runs over, the one named last changes fastest.
Arguments:
- query_vectors: bfloat16 [16, 16, 256, 1024], P('dp', 'sample'), may hold values from -6 to 6
- key_vectors: bfloat16 [16, 16, 256, 1024], P('dp', 'sample'), may hold values from -6 to 6
- value_vectors: bfloat16 [16, 16, 256, 2048], P('dp', 'sample'), may hold values from -6 to 6
- output_gates: bfloat16 [16, 16, 256, 2048], P('dp', 'sample'), may hold values from -6 to 6
- beta_logits: bfloat16 [16, 16, 16, 256], P('dp', 'sample'), may hold values from -6 to 6
- decay_logits: bfloat16 [16, 16, 16, 256], P('dp', 'sample'), may hold values from -6 to 6
- decay_rates: float32 [16], replicated, may hold values from 0.003 to 0.08
- norm_gain: float32 [128], replicated, may hold values from 0.5 to 1.5
- prefix_states: float32 [16, 16, 128, 128], P('dp', 'sample'), may hold values from -4 to 4
- cotangent: bfloat16 [16, 16, 256, 2048], P('dp', 'sample'), may hold values from -6 to 6
- rewards: float32 [16, 16], P('dp', 'sample'), may hold values from -4 to 4
- out_weight: float32 [2048, 2048], P('dp'), may hold values from -0.125 to 0.125
- first_moment: float32 [2048, 2048], P('dp'), may hold values from -4 to 4
- second_moment: float32 [2048, 2048], P('dp'), may hold values from 0.05 to 2
Outputs:
- prefix_grad: float32 [16, 16, 128, 128], P('dp', 'sample')
- weight_new: float32 [2048, 2048], P('dp')
- first_new: float32 [2048, 2048], P('dp')
- second_new: float32 [2048, 2048], P('dp')
All inputs are finite; a program needn't handle non-finite values.
Results may differ from a plain program's by a relative error of at most 0.0041.
Values may be sent and summed in bfloat16 or wider, within the bound.
A program may use at most 192 MiB of HBM per device.

v0:
```python
import jax
import jax.numpy as jnp
from jax import lax
from jax.sharding import PartitionSpec as P

SPAN = 64
LEN = 256


TOP_PRECISION = lax.Precision.HIGHEST


def unit_lower_solve(system, targets):
    block_width = system.shape[-1]
    result = targets - jnp.einsum("hij,hjc->hic", system, targets, precision=TOP_PRECISION)
    raised = system
    covered = 2
    while covered < block_width:
        raised = jnp.einsum("hij,hjk->hik", raised, raised, precision=TOP_PRECISION)
        result = result + jnp.einsum("hij,hjc->hic", raised, result, precision=TOP_PRECISION)
        covered = covered * 2
    return result


def span_step(carried_state, pieces):
    query_pieces, keys_c, values_c, beta_gates, decays_c = pieces
    block_width = query_pieces.shape[1]
    cumulative = jnp.cumsum(decays_c, axis=-1)
    row_index = lax.broadcasted_iota(jnp.int32, (block_width, block_width), 0)
    col_index = lax.broadcasted_iota(jnp.int32, (block_width, block_width), 1)
    causal = row_index >= col_index
    strictly = row_index > col_index
    spread = cumulative[:, :, None] - cumulative[:, None, :]
    falloff = jnp.where(causal, jnp.exp(jnp.where(causal, spread, 0.0)), 0.0)
    key_inner = jnp.einsum("hik,hjk->hij", keys_c, keys_c, precision=TOP_PRECISION)
    system = jnp.where(strictly, beta_gates[:, :, None] * key_inner * falloff, 0.0)
    decay_growth = jnp.exp(cumulative)
    targets = jnp.concatenate(
        [(beta_gates * decay_growth)[:, :, None] * keys_c, beta_gates[:, :, None] * values_c],
        axis=-1,
    )
    triangular_result = unit_lower_solve(system, targets)
    key_dimension = keys_c.shape[-1]
    corrected_values = triangular_result[..., key_dimension:] - jnp.einsum(
        "ale,aew->alw",
        triangular_result[..., :key_dimension],
        carried_state,
        precision=TOP_PRECISION,
    )
    scores = jnp.einsum("hik,hjk->hij", query_pieces, keys_c, precision=TOP_PRECISION) * falloff
    layer_output = jnp.einsum(
        "ale,aew->alw",
        query_pieces * decay_growth[:, :, None],
        carried_state,
        precision=TOP_PRECISION,
    )
    layer_output = layer_output + jnp.einsum(
        "hij,hjv->hiv", scores, corrected_values, precision=TOP_PRECISION
    )
    final_state = cumulative[:, -1:]
    decayed_keys = keys_c * jnp.exp(final_state - cumulative)[:, :, None]
    carried_state = jnp.exp(final_state)[:, :, None] * carried_state + jnp.einsum(
        "xnd,xnu->xdu", decayed_keys, corrected_values, precision=TOP_PRECISION
    )
    return (carried_state, layer_output)


def unit_vectors(source, head_count):
    shaped = source.astype(jnp.float32).reshape(source.shape[0], head_count, -1)
    return shaped * lax.rsqrt(jnp.sum(shaped * shaped, axis=-1, keepdims=True) + 1e-06)


def to_blocks(source, block_width):
    length, head_count, inner_width = source.shape
    return source.reshape(length // block_width, block_width, head_count, inner_width).transpose(
        0, 2, 1, 3
    )


def gate_blocks(source, block_width):
    head_count, length = source.shape
    return source.reshape(head_count, length // block_width, block_width).transpose(1, 0, 2)


def sequence_core(
    query_vectors, key_vectors, value_vectors, beta_logits, decay_logits, decay_rates, start_state
):
    head_count = beta_logits.shape[0]
    key_heads = head_count // 2
    length = query_vectors.shape[0]
    queries = unit_vectors(query_vectors, key_heads)
    queries = queries * queries.shape[-1] ** (-0.5)
    queries = jnp.repeat(queries, 2, axis=1)
    keys_unit = jnp.repeat(unit_vectors(key_vectors, key_heads), 2, axis=1)
    values_wide = value_vectors.astype(jnp.float32).reshape(length, head_count, -1)
    beta_gates = jax.nn.sigmoid(beta_logits.astype(jnp.float32))
    decays = -decay_rates[:, None] * jax.nn.softplus(decay_logits.astype(jnp.float32))
    pieces = (
        to_blocks(queries, SPAN),
        to_blocks(keys_unit, SPAN),
        to_blocks(values_wide, SPAN),
        gate_blocks(beta_gates, SPAN),
        gate_blocks(decays, SPAN),
    )
    closing_state, outputs = lax.scan(span_step, start_state, pieces)
    return outputs.transpose(0, 2, 1, 3).reshape(length, -1)


def gated_norm(core_in, output_gates, norm_gain):
    shaped = core_in.reshape(core_in.shape[:-1] + (-1, norm_gain.shape[0]))
    normed = (
        shaped * lax.rsqrt(jnp.mean(shaped * shaped, axis=-1, keepdims=True) + 1e-06) * norm_gain
    )
    return normed.reshape(core_in.shape) * jax.nn.silu(output_gates.astype(jnp.float32))


def adam_update(weight, first_moment, second_moment, gradient):
    first_new = 0.9 * first_moment + 0.1 * gradient
    second_new = 0.95 * second_moment + 0.05 * gradient * gradient
    direction = first_new / (1.0 - 0.9**10) / (jnp.sqrt(second_new / (1.0 - 0.95**10)) + 1e-08)
    weight_new = weight - 0.001 * (direction + 0.1 * weight)
    return (weight_new, first_new, second_new)


def local(
    query_vectors,
    key_vectors,
    value_vectors,
    output_gates,
    beta_logits,
    decay_logits,
    decay_rates,
    norm_gain,
    prefix_states,
    cotangent,
    rewards,
    out_weight,
    first_moment,
    second_moment,
):
    prompt_count, local_samples = rewards.shape
    sample_count = local_samples * lax.axis_size("sample")
    reward_sum = lax.psum(jnp.sum(rewards, axis=1), "sample")
    centre = (reward_sum / sample_count)[:, None]
    square_sum = lax.psum(jnp.sum((rewards - centre) * (rewards - centre), axis=1), "sample")
    variance = square_sum / sample_count
    spread = jnp.sqrt(variance)[:, None]
    coefficient = (rewards - centre) / jnp.maximum(spread, 0.6) / LEN
    weighted = (cotangent.astype(jnp.float32) * coefficient[:, :, None, None]).astype(jnp.bfloat16)
    start_states = lax.all_gather(prefix_states, "sample", axis=1, tiled=True)

    def merged(source):
        return source.reshape((-1,) + source.shape[2:])

    def run_local(start_in):
        spread_states = jnp.broadcast_to(
            start_in[:, None], (prompt_count, local_samples) + start_in.shape[1:]
        )
        return jax.vmap(sequence_core, in_axes=(0, 0, 0, 0, 0, None, 0))(
            merged(query_vectors),
            merged(key_vectors),
            merged(value_vectors),
            merged(beta_logits),
            merged(decay_logits),
            decay_rates,
            merged(spread_states),
        )

    core_out, pull_state = jax.vjp(run_local, start_states)
    flat_gates = merged(output_gates)
    mixed_wide, pull_norm = jax.vjp(
        lambda core_in: gated_norm(core_in, flat_gates, norm_gain), core_out
    )
    mixed_rows = mixed_wide.astype(jnp.bfloat16).reshape(-1, mixed_wide.shape[-1])
    flat_weighted = weighted.reshape(-1, weighted.shape[-1])
    back_rows = lax.dot_general(
        flat_weighted,
        lax.all_gather(out_weight.astype(jnp.bfloat16), "dp", axis=0, tiled=True),
        (((1,), (1,)), ((), ())),
        preferred_element_type=jnp.float32,
    )
    (core_grad,) = pull_norm(back_rows.reshape(core_out.shape))
    (start_grad,) = pull_state(core_grad)
    prefix_grad = lax.psum_scatter(start_grad, "sample", scatter_dimension=1, tiled=True)
    partial_rows = lax.psum_scatter(
        lax.dot_general(
            mixed_rows, flat_weighted, (((0,), (0,)), ((), ())), preferred_element_type=jnp.float32
        ),
        "dp",
        scatter_dimension=0,
        tiled=True,
    )
    gradient = lax.psum(partial_rows, "sample")
    weight_new, first_new, second_new = adam_update(
        out_weight, first_moment, second_moment, gradient
    )
    return (prefix_grad, weight_new, first_new, second_new)


def solution(mesh):
    placed = (
        P("dp", "sample", None, None),
        P("dp", "sample", None, None),
        P("dp", "sample", None, None),
        P("dp", "sample", None, None),
        P("dp", "sample", None, None),
        P("dp", "sample", None, None),
        P(),
        P(),
        P("dp", "sample", None, None),
        P("dp", "sample", None, None),
        P("dp", "sample"),
        P("dp", None),
        P("dp", None),
        P("dp", None),
    )
    return jax.shard_map(
        local,
        mesh=mesh,
        in_specs=placed,
        out_specs=(P("dp", "sample", None, None), P("dp", None), P("dp", None), P("dp", None)),
        check_vma=False,
    )
```

profile of v0, /device:TPU:0, one launch (start us, length us, event | category | flops | bytes accessed | tf_op | source)
XLA Modules:
  0.0 655.8 jit_solution(5685654636892577958)
XLA Ops:
  20.1 26.3 %psum.21 = f32[1]{0:T(128)} all-reduce(f32[1]{0:T(128)} %bitcast.9), channel_id=1, replica_groups=mesh['dp'=16,'sample'=8] {'sample'}, use_global_device_ids=true, to_apply=%region_1.0 | all-reduce | flops 1 | bytes 8 | tf_op jit(solution)/shard_map/psum | solution.py:143
  47.7 19.7 %psum.22 = f32[1]{0:T(128)} all-reduce(f32[1]{0:T(128)} %bitcast.11), channel_id=1, replica_groups=mesh['dp'=16,'sample'=8] {'sample'}, use_global_device_ids=true, to_apply=%region_3.0 | all-reduce | flops 1 | bytes 8 | tf_op jit(solution)/shard_map/psum | solution.py:145
  68.1 4.3 copy.55
  79.8 196.7 %while.41 = (s32[]{:T(128)}, f32[2,16,128,128]{3,2,1,0:T(8,128)S(1)}, f32[4,2,16,64,128]{4,3,2,1,0:T(8,128)}, f32[4,2,16,64,128]{4,3,2,1,0:T(8,128)}, f32[4,2,16...) while((s32[]{:T(128)}, ...), condition=%wide.region_8.9_spmd.clone.clone, body=%wide.region_6.8_spmd.clone.clone.sunk | while | flops 4739958784 | bytes 110893808 | solution.py:105
  137.5 4.1 multiply_add_fusion.5
  179.0 4.1 multiply_add_fusion.5
  220.5 4.1 multiply_add_fusion.5
  262.0 4.2 multiply_add_fusion.5
  276.5 9.3 %fusion.74 = f32[2,256,2048]{2,1,0:T(8,128)S(1)} fusion(bf16[2048,2048]{1,0:T(8,128)(2,1)} %all-gather.5.cloned.1.call-done, bf16[1,2,256,2048]{3,2,1,0:T(8,128)(2,1)} %multiply_convert_fusion, bf16[1,2,256,2048]{3,2,1,0:T(8,128)(2,1)} %param.21), kind=kOutput, calls=%fused_computation.103 | convolution fusion | flops 4301258752 | bytes 16777216 | tf_op jit(solution)/shard_map/dot_general | solution.py:176
  290.6 5.3 fusion.70
  297.5 8.3 %fusion.77 = f32[2048,2048]{1,0:T(8,128)} fusion(bf16[512,2048]{1,0:T(8,128)(2,1)S(1)} %bitcast.309, bf16[64,8,16,128]{3,2,1,0:T(8,128)(2,1)S(1)} %bitcast.310), kind=kOutput, calls=%fused_computation.106 | convolution fusion | flops 4294967296 | bytes 20971520 | tf_op jit(solution)/shard_map/dot_general | solution.py:186
  305.9 174.0 %reduce-scatter.5.cloned.1.call-done = f32[128,2048]{1,0:T(8,128)} async-done(((f32[2048,2048]{1,0:T(8,128)}), f32[128,2048]{1,0:T(8,128)}) %reduce-scatter.5.cloned.1.call-update) | async-done | bytes 1048592 | tf_op jit(solution)/shard_map/reduce_scatter | solution.py:185
  479.9 67.7 %while.42 = (s32[]{:T(128)}, f32[2,16,128,128]{3,2,1,0:T(8,128)S(1)}, f32[4,2,16,1,1]{2,1,4,3,0:T(2,128)S(1)}, f32[4,2,16,64,128]{4,3,2,1,0:T(8,128)}, f32[4,2,1...) while((s32[]{:T(128)}, ...), condition=%wide.region_12.13_spmd.clone, body=%wide.region_11.12_spmd.clone.sunk | while | flops 1412431872 | bytes 20974096 | solution.py:105
  480.2 3.4 fusion.225
  483.5 3.2 fusion.226
  486.8 5.0 fusion.224
  491.8 5.2 add_add_fusion.3
  497.0 3.4 fusion.225
  500.4 3.2 fusion.226
  503.6 5.0 fusion.224
  508.7 5.2 add_add_fusion.3
  513.9 3.4 fusion.225
  517.3 3.2 fusion.226
  520.5 5.0 fusion.224
  525.5 5.2 add_add_fusion.3
  530.8 3.4 fusion.225
  534.2 3.2 fusion.226
  537.4 5.0 fusion.224
  542.4 5.2 add_add_fusion.3
  548.9 26.4 %all-reduce.2.cloned.1.call-done = f32[128,2048]{1,0:T(8,128)} async-done(((f32[128,2048]{1,0:T(8,128)}), f32[128,2048]{1,0:T(8,128)}) %all-reduce.2.cloned.1.call-update) | async-done | bytes 1048592 | tf_op jit(solution)/shard_map/psum | solution.py:193
  575.3 4.1 multiply_subtract_fusion
  579.4 69.6 %reduce-scatter.3.cloned.1.call-done = f32[1,2,128,128]{3,2,1,0:T(8,128)} async-done(((f32[1,16,128,128]{3,2,1,0:T(8,128)}), f32[1,2,128,128]{3,2,1,0:T(8,128)}) %reduce-scatter.3.cloned.1.call-update) | async-done | bytes 131088 | tf_op jit(solution)/shard_map/reduce_scatter | solution.py:184
  (203 shorter events, 177.4 us)
Async XLA Ops:
  7.2 3.0 copy-start.9
  7.2 67.4 %all-gather.3.cloned.1.call-start = ((), (), s32[]{:S(2)}) async-start(), calls=%async_computation.2 | async-start | bytes 1179648 | tf_op jit(solution)/shard_map/all_gather | solution.py:150
  7.9 268.6 %all-gather.5.cloned.1.call-start = ((), (), s32[]{:S(2)}) async-start(), calls=%async_computation.3 | async-start | bytes 8912896 | tf_op jit(solution)/shard_map/all_gather | solution.py:178
  10.1 469.8 %reduce-scatter.5.cloned.1.call-start = ((), (), s32[]{:S(2)}) async-start(), calls=%async_computation.5 | async-start | bytes 17825792 | tf_op jit(solution)/shard_map/reduce_scatter | solution.py:185
  11.8 1.2 copy-start.10
  14.6 2.1 copy-start.6
  16.7 2.5 copy-start.12
  16.7 2.7 copy-start.16
  16.7 2.7 copy-start.13
  16.7 2.8 copy-start.15
  68.1 4.4 copy-start.7
  74.5 2.6 copy-start.4
  77.1 2.4 copy-start.11
  103.9 2.6 copy-start
  127.0 2.2 copy-start.1
  145.7 2.5 copy-start
  168.7 2.2 copy-start.1
  187.1 2.5 copy-start
  210.1 2.2 copy-start.1
  228.6 2.5 copy-start
  251.6 2.2 copy-start.1
  285.9 2.2 copy-start.3
  285.9 2.2 copy-start.14
  288.1 2.5 copy-start.2
  295.9 1.6 copy-start.8
  305.8 269.5 %all-reduce.2.cloned.1.call-start = ((), (), s32[]{:S(2)}) async-start(), calls=%async_computation.6 | async-start | bytes 2097152 | tf_op jit(solution)/shard_map/psum | solution.py:193
  479.9 169.2 %reduce-scatter.3.cloned.1.call-start = ((), (), s32[]{:S(2)}) async-start(), calls=%async_computation.4 | async-start | bytes 1179648 | tf_op jit(solution)/shard_map/reduce_scatter | solution.py:184
  547.7 27.7 %copy-start.5 = (f32[128,2048]{1,0:T(8,128)S(1)}, f32[128,2048]{1,0:T(8,128)}, u32[]{:S(2)}) copy-start(f32[128,2048]{1,0:T(8,128)} %param.29) | copy-start | bytes 3145732
Sparse Core Ops, SparseCore 0:
  10.4 48.9 all-gather.2
  61.6 50.8 all-gather.4
  306.0 173.8 reduce-scatter.4
  482.2 93.0 all-reduce.1
  579.3 69.6 reduce-scatter.2
where the time goes:
time: 662 us; the launch traced here: 656 us
  waiting for transfers between devices  271 us (41%)
  matrix products  220 us (33%)
  blocking collectives  46 us (7%)
  other arithmetic  38.8 us (6%)
  local copies, waits for them, and re-layouts  33.2 us (5%)
  loops' own time  31.4 us (5%)
  between operations  15.7 us (2%)
    reduce_scatter x1, waiting for transfers between devices, local(): lax.psum_scatter(lax.dot_general(mixed_rows, flat_weighted, (((0,), (0,))...  174 us
    reduce_scatter x1, waiting for transfers between devices, local(): lax.psum_scatter(start_grad, 'sample', scatter_dimension=1, tiled=True)  69.6 us
    dot_general x20, matrix products, unit_lower_solve(): jnp.einsum('hij,hjc->hic', raised, result, precision=TOP_PRECISION)  42.4 us
    another operation x2, loops' own time, sequence_core(): closing_state, outputs = lax.scan(span_step, start_state, pieces)  31.4 us
    dot_general x8, matrix products, span_step(): jnp.einsum('xnd,xnu->xdu', decayed_keys, corrected_values, precision=TOP_...  29.5 us
    dot_general x8, matrix products, span_step(): jnp.einsum('ale,aew->alw', triangular_result[..., :key_dimension], carrie...  29.1 us
    dot_general x8, matrix products, span_step(): jnp.einsum('ale,aew->alw', query_pieces * decay_growth[:, :, None], carri...  28.3 us
    psum x1, waiting for transfers between devices, local(): gradient = lax.psum(partial_rows, 'sample')  26.4 us
  transfers between devices with their start and end apart: 5, of which 3 were waited for; matrix products, arithmetic and copies ran while one was open for 39% of the time, Pallas kernels for 0%

commit v1 on v0

v1 whole, which is shorter than its diff:
```python
import functools
import jax
import jax.numpy as jnp
from jax import lax
from jax.experimental import pallas as pl
from jax.experimental.pallas import tpu as pltpu
from jax.sharding import PartitionSpec as P

LEN = 256
F32 = jnp.float32
BF = jnp.bfloat16


def dot(a, b, dims=((1,), (0,))):
    return lax.dot_general(a, b, (dims, ((), ())), preferred_element_type=F32)


def iota(shape, dim):
    return lax.broadcasted_iota(jnp.int32, shape, dim)


def split(x):
    high = x.astype(BF)
    return high, (x - high.astype(F32)).astype(BF)


def odd_rows(x, width):
    n = x.shape[0] // (2 * width)
    return x.reshape((n, 2, width) + x.shape[1:])[:, 1].reshape((n * width,) + x.shape[1:])


def put_odd(x, rows, width):
    n = x.shape[0] // (2 * width)
    parted = x.reshape((n, 2, width) + x.shape[1:])
    rows = rows.reshape((n, width) + x.shape[1:])
    return jnp.stack([parted[:, 0], parted[:, 1] - rows], axis=1).reshape(x.shape)


def inverses(systems, masks_ref):
    count = len(systems)
    eye = masks_ref[8]
    results = [eye - a * masks_ref[0] for a in systems]
    for level in range(1, 8):
        width = 1 << level
        mask = masks_ref[level]
        if width < 16:
            lefts = [dot(results[i], systems[i] * mask).astype(BF) for i in range(count)]
            fixes = [dot(lefts[i], results[i]).astype(BF) for i in range(count)]
            results = [results[i] - fixes[i] for i in range(count)]
        else:
            lefts = [dot(odd_rows(results[i], width), systems[i] * mask).astype(BF) for i in range(count)]
            fixes = [dot(lefts[i], results[i]).astype(BF) for i in range(count)]
            results = [put_odd(results[i], fixes[i], width) for i in range(count)]
    return [r - eye for r in results]


def forward_kernel(samples, q_ref, k_ref, v_ref, g_ref, small_ref, gain_ref, state_ref, mixed_ref, core_ref, read_ref, masks_ref):
    rows = iota((LEN, LEN), 0)
    cols = iota((LEN, LEN), 1)

    @pl.when(pl.program_id(0) == 0)
    def _():
        for level in range(8):
            same = (rows >> (level + 1)) == (cols >> (level + 1))
            below = (rows >> level) > (cols >> level)
            masks_ref[level] = jnp.where(same & below, 1.0, 0.0).astype(BF)
        masks_ref[8] = jnp.where(rows == cols, 1.0, 0.0).astype(BF)
        masks_ref[9] = jnp.where(rows <= cols, 1.0, 0.0).astype(BF)

    small = small_ref[0]
    first = small.astype(BF)
    rest = small - first.astype(F32)
    second = rest.astype(BF)
    third = (rest - second.astype(F32)).astype(BF)
    upper = masks_ref[9]
    running = dot(first, upper) + dot(second, upper) + dot(third, upper)
    mixed_small = jnp.where(iota(small.shape, 0) < 2 * samples, jax.nn.sigmoid(small), running)
    columns = mixed_small.T
    causal = rows >= cols
    strict = rows > cols
    diagonal = rows == cols
    gain = gain_ref[...]

    systems, scores, gates, rights, queries = [], [], [], [], []
    for s in range(samples):
        q = q_ref[s]
        k = k_ref[s]
        qk = dot(jnp.concatenate([k, q], axis=0), k, ((1,), (1,)))
        kk, qk = qk[:LEN], qk[LEN:]
        kf = k.astype(F32)
        qf = q.astype(F32)
        k_row = lax.rsqrt(jnp.sum(jnp.where(diagonal, kk, 0.0), axis=0, keepdims=True) + 1e-6)
        k_col = lax.rsqrt(jnp.sum(kf * kf, axis=1, keepdims=True) + 1e-6)
        q_col = lax.rsqrt(jnp.sum(qf * qf, axis=1, keepdims=True) + 1e-6) * (128 ** -0.5)
        kk = kk * k_row
        qk = qk * k_row
        for r in range(2):
            i = 2 * s + r
            beta = columns[:, i:i + 1]
            c_col = columns[:, 2 * samples + i:2 * samples + i + 1]
            c_row = mixed_small[2 * samples + i:2 * samples + i + 1]
            falloff = jnp.exp(jnp.where(causal, c_col - c_row, 0.0))
            a = jnp.where(strict, falloff * kk * (beta * k_col), 0.0)
            p = jnp.where(causal, falloff * qk * q_col, 0.0)
            growth = jnp.exp(c_col)
            v = v_ref[s, :, 128 * r:128 * r + 128].astype(F32)
            systems.append(a.astype(BF))
            scores.append(split(p))
            rights.append(jnp.concatenate([beta * v, (beta * growth * k_col) * kf], axis=1))
            queries.append((growth * q_col) * qf)
    solved = inverses(systems, masks_ref)
    for s in range(samples):
        for r in range(2):
            i = 2 * s + r
            u = rights[i] + dot(solved[i], rights[i].astype(BF))
            u_high, u_low = split(u)
            p_high, p_low = scores[i]
            pu = dot(p_high, u_high) + (dot(p_low, u_high) + dot(p_high, u_low))
            read = queries[i] - pu[:, 128:]
            read16 = read.astype(BF)
            core = pu[:, :128] + dot(read16, state_ref[r].astype(BF))
            gate = g_ref[s, :, 128 * r:128 * r + 128].astype(F32)
            scale = lax.rsqrt(jnp.mean(core * core, axis=1, keepdims=True) + 1e-6)
            mixed_ref[s, :, 128 * r:128 * r + 128] = (core * scale * gain * (gate * jax.nn.sigmoid(gate))).astype(BF)
            core_ref[s, :, 128 * r:128 * r + 128] = core.astype(BF)
            read_ref[s, :, 128 * r:128 * r + 128] = read16


def forward(q, k, v, g, small, gain, state, samples=2):
    kheads = q.shape[2] // 128
    wide = pl.BlockSpec((samples, LEN, 256), lambda i: (0, 0, i))
    narrow = pl.BlockSpec((samples, LEN, 128), lambda i: (0, 0, i))
    out = jax.ShapeDtypeStruct((samples, LEN, kheads * 256), BF)
    return pl.pallas_call(
        functools.partial(forward_kernel, samples),
        grid=(kheads,),
        in_specs=[
            narrow, narrow, wide, wide,
            pl.BlockSpec((1, 4 * samples, LEN), lambda i: (i, 0, 0)),
            pl.BlockSpec((1, 128), lambda i: (0, 0)),
            pl.BlockSpec((2, 128, 128), lambda i: (i, 0, 0)),
        ],
        out_specs=[wide, wide, wide],
        out_shape=[out, out, out],
        scratch_shapes=[pltpu.VMEM((10, LEN, LEN), BF)],
        compiler_params=pltpu.CompilerParams(vmem_limit_bytes=48 * 1024 * 1024),
        cost_estimate=pl.CostEstimate(flops=16_000_000_000, bytes_accessed=14_000_000, transcendentals=0),
    )(q, k, v, g, small, gain, state)


def backward_kernel(samples, back_ref, g_ref, core_ref, read_ref, gain_ref, out_ref):
    gain = gain_ref[...]
    total = jnp.zeros((128, 128), F32)
    for s in range(samples):
        core = core_ref[s].astype(F32)
        gate = g_ref[s].astype(F32)
        scale = lax.rsqrt(jnp.mean(core * core, axis=1, keepdims=True) + 1e-6)
        normed = core * scale
        lifted = back_ref[s] * gain * (gate * jax.nn.sigmoid(gate))
        core_grad = scale * (lifted - normed * jnp.mean(lifted * normed, axis=1, keepdims=True))
        total = total + dot(read_ref[s], core_grad.astype(BF), ((0,), (0,)))
    out_ref[0] = total


def backward(back, g, core, read, gain, samples=2):
    heads = g.shape[2] // 128
    block = pl.BlockSpec((samples, LEN, 128), lambda i: (0, 0, i))
    return pl.pallas_call(
        functools.partial(backward_kernel, samples),
        grid=(heads,),
        in_specs=[block, block, block, block, pl.BlockSpec((1, 128), lambda i: (0, 0))],
        out_specs=pl.BlockSpec((1, 128, 128), lambda i: (i, 0, 0)),
        out_shape=jax.ShapeDtypeStruct((heads, 128, 128), F32),
        compiler_params=pltpu.CompilerParams(vmem_limit_bytes=48 * 1024 * 1024),
        cost_estimate=pl.CostEstimate(flops=500_000_000, bytes_accessed=12_000_000, transcendentals=0),
    )(back, g, core, read, gain)


def adam_update(weight, first_moment, second_moment, gradient):
    first_new = 0.9 * first_moment + 0.1 * gradient
    second_new = 0.95 * second_moment + 0.05 * gradient * gradient
    direction = first_new / (1.0 - 0.9**10) / (jnp.sqrt(second_new / (1.0 - 0.95**10)) + 1e-08)
    weight_new = weight - 0.001 * (direction + 0.1 * weight)
    return (weight_new, first_new, second_new)


def local(
    query_vectors,
    key_vectors,
    value_vectors,
    output_gates,
    beta_logits,
    decay_logits,
    decay_rates,
    norm_gain,
    prefix_states,
    cotangent,
    rewards,
    out_weight,
    first_moment,
    second_moment,
):
    samples = rewards.shape[1]
    heads = beta_logits.shape[2]
    all_rewards = lax.all_gather(rewards, "sample", axis=1, tiled=True)
    centre = jnp.mean(all_rewards, axis=1, keepdims=True)
    spread = jnp.sqrt(jnp.mean((all_rewards - centre) * (all_rewards - centre), axis=1, keepdims=True))
    coefficient = (rewards - centre) / jnp.maximum(spread, 0.6) / LEN
    weighted = (cotangent[0].astype(F32) * coefficient[0, :, None, None]).astype(BF)
    states = lax.all_gather(prefix_states[0], "sample", axis=0, tiled=True)
    weight16 = lax.all_gather(out_weight.astype(BF), "dp", axis=0, tiled=True)
    decays = -decay_rates[:, None] * jax.nn.softplus(decay_logits[0].astype(F32))

    def by_pair(x):
        return x.reshape(samples, heads // 2, 2, LEN).transpose(1, 0, 2, 3).reshape(heads // 2, 2 * samples, LEN)

    small = jnp.concatenate([by_pair(beta_logits[0].astype(F32)), by_pair(decays)], axis=1)
    gain = norm_gain[None]
    gates = output_gates[0]
    mixed, core, read = forward(
        query_vectors[0], key_vectors[0], value_vectors[0], gates, small, gain, states, samples
    )
    flat_weighted = weighted.reshape(-1, weighted.shape[-1])
    partial = lax.dot_general(
        mixed.reshape(-1, mixed.shape[-1]), flat_weighted, (((0,), (0,)), ((), ())), preferred_element_type=F32
    ).astype(BF)
    partial_rows = lax.psum_scatter(partial, "dp", scatter_dimension=0, tiled=True)
    back = lax.dot_general(
        flat_weighted, weight16, (((1,), (1,)), ((), ())), preferred_element_type=F32
    ).reshape(samples, LEN, -1)
    start_grad = backward(back, gates, core, read, gain, samples)
    prefix_grad = lax.psum_scatter(start_grad, "sample", scatter_dimension=0, tiled=True)[None]
    gradient = lax.psum(partial_rows.astype(F32), "sample")
    return (prefix_grad,) + adam_update(out_weight, first_moment, second_moment, gradient)


def solution(mesh):
    placed = (
        P("dp", "sample", None, None),
        P("dp", "sample", None, None),
        P("dp", "sample", None, None),
        P("dp", "sample", None, None),
        P("dp", "sample", None, None),
        P("dp", "sample", None, None),
        P(),
        P(),
        P("dp", "sample", None, None),
        P("dp", "sample", None, None),
        P("dp", "sample"),
        P("dp", None),
        P("dp", None),
        P("dp", None),
    )
    return jax.shard_map(
        local,
        mesh=mesh,
        in_specs=placed,
        out_specs=(P("dp", "sample", None, None), P("dp", None), P("dp", None), P("dp", None)),
        check_vma=False,
    )
```

time: 662 us -> 446 us (0.67)
  matrix products: 220 us -> 17.6 us
  blocking collectives: 46 us -> 105 us
  Pallas kernels: 0 us -> 56 us
  waiting for transfers between devices: 271 us -> 236 us
  other arithmetic: 38.8 us -> 6.26 us
  loops' own time: 31.4 us -> 0 us
  local copies, waits for them, and re-layouts: 33.2 us -> 8.04 us
    dot_general x86 -> x2, matrix products: 220 us -> 17.6 us  [the longest x1 10.7 us: local(): lax.dot_general(flat_weighted, weight16, (((1,), (1,)), ((), ())), prefer...]
    reduce_scatter x2, waiting for transfers between devices: 244 us -> 166 us  [the longest x1 93.2 us: local(): lax.psum_scatter(partial, 'dp', scatter_dimension=0, tiled=True)]
    all_gather x2, waiting for transfers between devices: 0.02 us -> 68.7 us  [the longest x1 51.4 us: local(): weight16 = lax.all_gather(out_weight.astype(BF), 'dp', axis=0, tiled=True)]
    pallas_call x0 -> x2, Pallas kernels: none -> 56 us  [the longest x1 43.1 us: forward(): pl.pallas_call(functools.partial(forward_kernel, samples), grid=(kheads,)...]
    psum x2 -> x1, blocking collectives: 46 us -> 79.6 us  [local(): gradient = lax.psum(partial_rows.astype(F32), 'sample')]
    another operation x2 -> x0, loops' own time: 31.4 us -> none  [sequence_core(): closing_state, outputs = lax.scan(span_step, start_state, pieces)]
    psum x1 -> x0, waiting for transfers between devices: 26.4 us -> none  [local(): gradient = lax.psum(partial_rows, 'sample')]
    unnamed x0 -> x1, blocking collectives: none -> 25.7 us
  transfers between devices with their start and end apart: 5 -> 4, of which waited for: 3 -> 4; matrix products, arithmetic and copies ran while one was open for 39% -> 1% of each run, Pallas kernels for 0% -> 0%
where the time goes in v1:
time: 446 us; the launch traced here: 445 us
  waiting for transfers between devices  236 us (53%)
  blocking collectives  105 us (24%)
  Pallas kernels  56 us (13%)
  matrix products  17.6 us (4%)
  between operations  15.9 us (4%)
  local copies, waits for them, and re-layouts  8.04 us (2%)
  other arithmetic  6.26 us (1%)
    reduce_scatter x1, waiting for transfers between devices, local(): lax.psum_scatter(partial, 'dp', scatter_dimension=0, tiled=True)  93.2 us
    psum x1, blocking collectives, local(): gradient = lax.psum(partial_rows.astype(F32), 'sample')  79.6 us
    reduce_scatter x1, waiting for transfers between devices, local(): lax.psum_scatter(start_grad, 'sample', scatter_dimension=0, tiled=True)  72.9 us
    all_gather x1, waiting for transfers between devices, local(): weight16 = lax.all_gather(out_weight.astype(BF), 'dp', axis=0, tiled=True)  51.4 us
    pallas_call x1, Pallas kernels, forward(): pl.pallas_call(functools.partial(forward_kernel, samples), grid=(kheads,)...  43.1 us
    unnamed x1, blocking collectives  25.7 us
    all_gather x1, waiting for transfers between devices, local(): states = lax.all_gather(prefix_states[0], 'sample', axis=0, tiled=True)  17.3 us
    pallas_call x1, Pallas kernels, backward(): pl.pallas_call(functools.partial(backward_kernel, samples), grid=(heads,)...  12.9 us
  transfers between devices with their start and end apart: 4, of which 4 were waited for; matrix products, arithmetic and copies ran while one was open for 1% of the time, Pallas kernels for 0%

profile of v1, /device:TPU:0, one launch (start us, length us, event | category | flops | bytes accessed | tf_op | source)
XLA Modules:
  0.0 445.1 jit_solution(5759128328086467601)
XLA Ops:
  7.2 0.0 all-gather.6.cloned.1.call-start
  7.2 0.7 all-gather.6.cloned.1.call-update
  7.9 0.0 reduce-scatter.5.cloned.1.call-start
  8.0 0.7 neg.9
  8.6 1.2 dynamic-slice
  10.5 0.8 bitcast_dynamic-update-slice_fusion
  11.3 25.7 %all-reduce = f32[16]{0:T(128)S(1)} all-reduce(f32[16]{0:T(128)S(1)} %bitcast_dynamic-update-slice_fusion), channel_id=1, replica_groups=mesh['dp'=16,'sample'=8] {'sample'}, use_global_device_ids=true, to_apply=%add | all-reduce | flops 16 | bytes 128
  37.0 0.6 reduce_sum.18
  38.3 0.6 multiply_reduce_fusion
  39.6 0.1 mul.63
  39.6 0.1 copy.46
  39.7 0.7 reshape.73
  40.5 0.7 copy.47
  41.3 0.1 fusion.6
  41.4 0.7 multiply_bitcast_fusion
  42.0 17.3 %all-gather.6.cloned.1.call-done = f32[1,16,128,128]{3,2,0,1:T(8,128)} async-done(((f32[1,2,128,128]{3,2,0,1:T(8,128)}), f32[1,16,128,128]{3,2,0,1:T(8,128)}) %all-gather.6.cloned.1.call-update) | async-done | bytes 1048592 | tf_op jit(solution)/shard_map/all_gather | solution.py:210
  59.3 0.7 copy-done.2
  60.0 1.2 copy-done.4
  61.2 1.2 copy-done.5
  62.4 1.2 copy-done.6
  63.7 43.1 %shard_map.165 = (bf16[2,256,2048]{2,1,0:T(8,128)(2,1)S(1)}, bf16[2,256,2048]{2,1,0:T(8,128)(2,1)}, bf16[2,256,2048]{2,1,0:T(8,128)(2,1)}) custom-call(bf16[2,256,1024]{2,1,0:T(8,128)(2,1)S(1)} %bitcast.37, bf16[2,256,1024]{2,1,0:T(8,128)(2,1)S(1)} %bitcast.38, bf16[2,256,2048]{2,1,0:T(8,128)(2,1)} %bitcast.44, bf16[2,256,2048]{2,1,0:T(8,128)(2,1)} %bitcast.33, ...), custom_call_target="tpu_custom_call" | custom-call | flops 16000000000 | bytes 14000000 | tf_op jit(solution)/shard_map/pallas_call | solution.py:134
  106.8 6.9 %bitcast_convert_fusion = bf16[2048,2048]{1,0:T(8,128)(2,1)} fusion(bf16[2,256,2048]{2,1,0:T(8,128)(2,1)S(1)} %get-tuple-element.9, bf16[1,2,256,2048]{3,2,1,0:T(8,128)(2,1)S(1)} %copy-done.9, f32[2]{0:T(128)S(1)} %multiply_bitcast_fusion), kind=kOutput, calls=%fused_computation | convolution fusion | flops 4302307328 | bytes 12582920 | tf_op jit(solution)/shard_map/dot_general | solution.py:224
  113.8 0.0 all-gather.4.cloned.1.call-start
  113.8 93.2 %reduce-scatter.5.cloned.1.call-done = bf16[128,2048]{1,0:T(8,128)(2,1)} async-done(((bf16[2048,2048]{1,0:T(8,128)(2,1)}), bf16[128,2048]{1,0:T(8,128)(2,1)}) %reduce-scatter.5.cloned.1.call-update) | async-done | bytes 524304 | tf_op jit(solution)/shard_map/reduce_scatter | solution.py:227
  207.0 79.6 %all-reduce.2 = f32[128,2048]{1,0:T(8,128)S(1)} all-reduce(bf16[128,2048]{1,0:T(8,128)(2,1)} %reduce-scatter.5.cloned.1.call-done), channel_id=1, replica_groups=mesh['dp'=16,'sample'=8] {'sample'}, use_global_device_ids=true, to_apply=%region_4.5 | all-reduce | flops 262144 | bytes 1572864 | tf_op jit(solution)/shard_map/psum | solution.py:233
  286.7 3.6 multiply_subtract_fusion
  290.3 0.0 all-gather.4.cloned.1.call-update
  290.4 0.2 reduce-scatter.3.cloned.1.call-start
  290.6 51.4 %all-gather.4.cloned.1.call-done = bf16[2048,2048]{1,0:T(8,128)(2,1)} async-done(((bf16[128,2048]{1,0:T(8,128)(2,1)}), bf16[2048,2048]{1,0:T(8,128)(2,1)}) %all-gather.4.cloned.1.call-update) | async-done | bytes 8388624 | tf_op jit(solution)/shard_map/all_gather | solution.py:211
  342.1 10.7 %fusion.back_ref = f32[2,256,2048]{2,1,0:T(8,128)} fusion(bf16[2048,2048]{1,0:T(8,128)(2,1)} %all-gather.4.cloned.1.call-done, bf16[1,2,256,2048]{3,2,1,0:T(8,128)(2,1)} %param.23, f32[2]{0:T(128)S(1)} %multiply_bitcast_fusion), kind=kOutput, calls=%fused_computation.1 | convolution fusion | flops 4298113024 | bytes 14680072 | tf_op jit(solution)/shard_map/dot_general | solution.py:228
  352.7 12.9 %shard_map.166 = f32[16,128,128]{2,1,0:T(8,128)} custom-call(f32[2,256,2048]{2,1,0:T(8,128)} %fusion.back_ref, bf16[2,256,2048]{2,1,0:T(8,128)(2,1)S(1)} %bitcast.34, bf16[2,256,2048]{2,1,0:T(8,128)(2,1)S(1)} %copy-done.1, bf16[2,256,2048]{2,1,0:T(8,128)(2,1)} %get-tuple-element.8.read_ref, f32[1,128]{1,0:T(1,128)S(1)} %bitcast.36), custom_call_target="tpu_custom_call" | custom-call | flops 500000000 | bytes 12000000 | tf_op jit(solution)/shard_map/pallas_call | solution.py:168
  365.7 72.9 %reduce-scatter.3.cloned.1.call-done = f32[2,128,128]{2,1,0:T(8,128)} async-done(((f32[16,128,128]{2,1,0:T(8,128)}), f32[2,128,128]{2,1,0:T(8,128)}) %reduce-scatter.3.cloned.1.call-update) | async-done | bytes 131088 | tf_op jit(solution)/shard_map/reduce_scatter | solution.py:232
  (23 shorter events, 0.1 us)
Async XLA Ops:
  7.2 52.2 %all-gather.6.cloned.1.call-start = ((), (), s32[]{:S(2)}) async-start(), calls=%async_computation.5 | async-start | bytes 1179648 | tf_op jit(solution)/shard_map/all_gather | solution.py:210
  7.9 199.1 %reduce-scatter.5.cloned.1.call-start = ((), (), s32[]{:S(2)}) async-start(), calls=%async_computation.4 | async-start | bytes 8912896 | tf_op jit(solution)/shard_map/reduce_scatter | solution.py:227
  59.3 0.7 copy-start.2
  60.0 1.2 copy-start.4
  61.2 1.2 copy-start.5
  62.4 1.2 copy-start.6
  63.7 43.1 %copy-start.9 = (bf16[1,2,256,2048]{3,2,1,0:T(8,128)(2,1)S(1)}, bf16[1,2,256,2048]{3,2,1,0:T(8,128)(2,1)}, u32[]{:S(2)}) copy-start(bf16[1,2,256,2048]{3,2,1,0:T(8,128)(2,1)} %param.23) | copy-start | bytes 6291460
  113.7 172.9 %copy-start.8 = (f32[128,2048]{1,0:T(8,128)S(1)}, f32[128,2048]{1,0:T(8,128)}, u32[]{:S(2)}) copy-start(f32[128,2048]{1,0:T(8,128)} %param.26) | copy-start | bytes 3145732
  113.8 172.9 %copy-start.7 = (f32[128,2048]{1,0:T(8,128)S(1)}, f32[128,2048]{1,0:T(8,128)}, u32[]{:S(2)}) copy-start(f32[128,2048]{1,0:T(8,128)} %param.25) | copy-start | bytes 3145732
  113.8 228.3 %all-gather.4.cloned.1.call-start = ((), (), s32[]{:S(2)}) async-start(), calls=%async_computation.2 | async-start | bytes 8912896 | tf_op jit(solution)/shard_map/all_gather | solution.py:211
  290.4 62.4 %copy-start = (bf16[1,2,256,2048]{3,2,1,0:T(8,128)(2,1)S(1)}, bf16[1,2,256,2048]{3,2,1,0:T(8,128)(2,1)}, u32[]{:S(2)}) copy-start(bf16[1,2,256,2048]{3,2,1,0:T(8,128)(2,1)} %param.17) | copy-start | bytes 6291460
  290.4 62.4 %copy-start.3 = (f32[128]{0:T(128)S(1)}, f32[128]{0:T(128)}, u32[]{:S(2)}) copy-start(f32[128]{0:T(128)} %param.21) | copy-start | bytes 1540
  290.4 148.2 %reduce-scatter.3.cloned.1.call-start = ((), (), s32[]{:S(2)}) async-start(), calls=%async_computation.3 | async-start | bytes 1179648 | tf_op jit(solution)/shard_map/reduce_scatter | solution.py:232
  342.1 10.7 %copy-start.1 = (bf16[2,256,2048]{2,1,0:T(8,128)(2,1)S(1)}, bf16[2,256,2048]{2,1,0:T(8,128)(2,1)}, u32[]{:S(2)}) copy-start(bf16[2,256,2048]{2,1,0:T(8,128)(2,1)} %get-tuple-element.7.core_ref) | copy-start | bytes 6291460
Sparse Core Ops, SparseCore 0:
  10.4 48.9 all-gather.5
  113.9 93.1 reduce-scatter.4
  290.5 51.5 all-gather.3
  365.8 72.7 reduce-scatter.2

commit v2 on v1

v2 whole, which is shorter than its diff:
```python
import functools
import jax
import jax.numpy as jnp
from jax import lax
from jax.experimental import pallas as pl
from jax.experimental.pallas import tpu as pltpu
from jax.sharding import PartitionSpec as P

LEN = 256
F32 = jnp.float32
BF = jnp.bfloat16
MESH = pl.DeviceIdType.MESH
CHIPS = 8
GROUP = 8


def dot(a, b, dims=((1,), (0,))):
    return lax.dot_general(a, b, (dims, ((), ())), preferred_element_type=F32)


def iota(shape, dim):
    return lax.broadcasted_iota(jnp.int32, shape, dim)


def split(x):
    high = x.astype(BF)
    return high, (x - high.astype(F32)).astype(BF)


def odd_rows(x, width):
    n = x.shape[0] // (2 * width)
    return x.reshape((n, 2, width) + x.shape[1:])[:, 1].reshape((n * width,) + x.shape[1:])


def put_odd(x, rows, width):
    n = x.shape[0] // (2 * width)
    parted = x.reshape((n, 2, width) + x.shape[1:])
    rows = rows.reshape((n, width) + x.shape[1:])
    return jnp.stack([parted[:, 0], parted[:, 1] - rows], axis=1).reshape(x.shape)


def inverses(systems, masks_ref):
    count = len(systems)
    eye = masks_ref[8]
    results = [eye - a * masks_ref[0] for a in systems]
    for level in range(1, 8):
        width = 1 << level
        mask = masks_ref[level]
        if width < 16:
            lefts = [dot(results[i], systems[i] * mask).astype(BF) for i in range(count)]
            fixes = [dot(lefts[i], results[i]).astype(BF) for i in range(count)]
            results = [results[i] - fixes[i] for i in range(count)]
        else:
            lefts = [dot(odd_rows(results[i], width), systems[i] * mask).astype(BF) for i in range(count)]
            fixes = [dot(lefts[i], results[i]).astype(BF) for i in range(count)]
            results = [put_odd(results[i], fixes[i], width) for i in range(count)]
    return [r - eye for r in results]


def places():
    dp = lax.axis_index("dp")
    return lax.div(dp, 4), lax.rem(lax.div(dp, 2), 2), lax.rem(dp, 2), lax.axis_index("sample")


def remote(src, dst, send, recv, where):
    return pltpu.make_async_remote_copy(
        src_ref=src, dst_ref=dst, send_sem=send, recv_sem=recv, device_id=where, device_id_type=MESH
    )


def greet(partners):
    barrier = pltpu.get_barrier_semaphore()
    for partner in partners:
        pl.semaphore_signal(barrier, inc=1, device_id=partner, device_id_type=MESH)
    pl.semaphore_wait(barrier, len(partners))


def lane_block(index, width):
    return pl.ds(pl.multiple_of(index * width, width), width)


def first_kernel(
    samples, q_ref, k_ref, v_ref, g_ref, small_ref, gain_ref, state_ref, reward_ref, cot_ref, weight_ref,
    core_ref, read_ref, weighted_ref, part_ref, all_ref,
    masks_ref, states_ref, rewards_ref, mixed_ref, other_ref, weighted_other_ref, gsend_ref, grecv_ref, acc_ref,
    st_send, st_recv, rw_send, rw_recv, wt_send, wt_recv, mx_send, mx_recv, g_send, g_recv,
    w1_send, w1_recv, w2_send, w2_recv, w3_send, w3_recv, w4_send, w4_recv, local_sem,
):
    x, yl, core_id, me = places()
    chip = x * 2 + yl
    sibling = {"dp": chip * 2 + 1 - core_id, "sample": me}

    def at_chip(index):
        return {"dp": index * 2 + core_id, "sample": me}

    def in_group(offset):
        return {"sample": lax.rem(me + offset, GROUP)}

    y_hi, z = lax.div(me, 4), lax.rem(me, 4)
    far = (1 - y_hi) * 4 + z

    def z_peer(offset):
        return {"sample": y_hi * 4 + lax.rem(z + offset, 4)}

    chip_peers = []
    for t in range(1, CHIPS):
        chip_peers.append(lax.rem(x + t // 2, 4) * 2 + lax.rem(yl + t % 2, 2))
    group_peers = [in_group(o) for o in range(1, GROUP)]
    greet([sibling] + [at_chip(c) for c in chip_peers] + group_peers)

    st_copies = [remote(state_ref, states_ref.at[me], st_send.at[o], st_recv.at[o], group_peers[o]) for o in range(GROUP - 1)]
    rw_copies = [remote(reward_ref, rewards_ref.at[me], rw_send.at[o], rw_recv.at[o], group_peers[o]) for o in range(GROUP - 1)]
    for copy in st_copies + rw_copies:
        copy.start()
    mine = all_ref.at[me, core_id, lane_block(chip, 128)]
    w1_copies = [remote(weight_ref.at[me], mine, w1_send.at[t], w1_recv.at[t], at_chip(chip_peers[t])) for t in range(CHIPS - 1)]
    for copy in w1_copies:
        copy.start()
    own = pltpu.make_async_copy(weight_ref.at[me], mine, local_sem)
    own.start()
    states_ref[me] = state_ref[...]
    rewards_ref[me] = reward_ref[...]

    held = all_ref.at[me, core_id]
    far_held = all_ref.at[far, core_id]
    w2_copy = remote(held, held, w2_send, w2_recv, {"sample": far})
    w3_copies = [remote(held, held, w3_send.at[o], w3_recv.at[o], z_peer(o + 1)) for o in range(3)]
    w3_far = [remote(far_held, far_held, w3_send.at[3 + o], w3_recv.at[3 + o], z_peer(o + 1)) for o in range(3)]

    def shared(index, slot):
        piece = all_ref.at[index, core_id]
        return remote(piece, piece, w4_send.at[slot], w4_recv.at[slot], sibling)

    def came(offset):
        return y_hi * 4 + lax.rem(z + 4 - offset, 4)

    def came_far(offset):
        return (1 - y_hi) * 4 + lax.rem(z + 4 - offset, 4)

    w4_copies = [shared(me, 0), shared(far, 1)]
    w4_copies += [shared(came(o + 1), 2 + o) for o in range(3)]
    w4_copies += [shared(came_far(o + 1), 5 + o) for o in range(3)]

    rows = iota((LEN, LEN), 0)
    cols = iota((LEN, LEN), 1)
    for level in range(8):
        same = (rows >> (level + 1)) == (cols >> (level + 1))
        below = (rows >> level) > (cols >> level)
        masks_ref[level] = jnp.where(same & below, 1.0, 0.0).astype(BF)
    masks_ref[8] = jnp.where(rows == cols, 1.0, 0.0).astype(BF)
    masks_ref[9] = jnp.where(rows <= cols, 1.0, 0.0).astype(BF)
    gain = gain_ref[...]

    def pair_at(t):
        return lax.rem(x + 3 - lax.div(t, 2), 4) * 2 + lax.rem(yl + 1 - lax.rem(t, 2), 2)

    wt_copy = remote(weighted_ref, weighted_other_ref, wt_send, wt_recv, sibling)

    def mixed_copy(t):
        return remote(mixed_ref.at[t, 1 - core_id], other_ref.at[t], mx_send.at[t], mx_recv.at[t], sibling)

    def to_row(t):
        target = lax.rem(x + 3 - lax.div(t, 2), 4) * 2 + yl
        return remote(gsend_ref.at[t], grecv_ref.at[t], g_send.at[t], g_recv.at[t], at_chip(target))

    to_column = remote(gsend_ref.at[6], grecv_ref.at[6], g_send.at[6], g_recv.at[6], at_chip(x * 2 + 1 - yl))

    def forward_step(t):
        pair = pair_at(t)
        small = small_ref[pair]
        first = small.astype(BF)
        rest = small - first.astype(F32)
        second = rest.astype(BF)
        third = (rest - second.astype(F32)).astype(BF)
        upper = masks_ref[9]
        running = dot(first, upper) + dot(second, upper) + dot(third, upper)
        by_row = jnp.where(iota(small.shape, 0) < 2 * samples, jax.nn.sigmoid(small), running)
        columns = by_row.T
        causal = rows >= cols
        strict = rows > cols
        diagonal = rows == cols
        systems, scores, rights, queries = [], [], [], []
        for s in range(samples):
            q = q_ref[s, :, lane_block(pair, 128)]
            k = k_ref[s, :, lane_block(pair, 128)]
            qk = dot(jnp.concatenate([k, q], axis=0), k, ((1,), (1,)))
            kk, qk = qk[:LEN], qk[LEN:]
            kf = k.astype(F32)
            qf = q.astype(F32)
            k_row = lax.rsqrt(jnp.sum(jnp.where(diagonal, kk, 0.0), axis=0, keepdims=True) + 1e-6)
            k_col = lax.rsqrt(jnp.sum(kf * kf, axis=1, keepdims=True) + 1e-6)
            q_col = lax.rsqrt(jnp.sum(qf * qf, axis=1, keepdims=True) + 1e-6) * (128 ** -0.5)
            kk = kk * k_row
            qk = qk * k_row
            v = v_ref[s, :, lane_block(pair, 256)].astype(F32)
            for r in range(2):
                i = 2 * s + r
                beta = columns[:, i:i + 1]
                c_col = columns[:, 2 * samples + i:2 * samples + i + 1]
                c_row = by_row[2 * samples + i:2 * samples + i + 1]
                falloff = jnp.exp(jnp.where(causal, c_col - c_row, 0.0))
                a = jnp.where(strict, falloff * kk * (beta * k_col), 0.0)
                p = jnp.where(causal, falloff * qk * q_col, 0.0)
                growth = jnp.exp(c_col)
                systems.append(a.astype(BF))
                scores.append(split(p))
                rights.append(
                    jnp.concatenate([beta * v[:, 128 * r:128 * r + 128], (beta * growth * k_col) * kf], axis=1)
                )
                queries.append((growth * q_col) * qf)
        solved = inverses(systems, masks_ref)

        @pl.when(t == 0)
        def _():
            for copy in st_copies:
                copy.wait()

        for s in range(samples):
            gates = g_ref[s, :, lane_block(pair, 256)].astype(F32)
            for r in range(2):
                i = 2 * s + r
                u = rights[i] + dot(solved[i], rights[i].astype(BF))
                u_high, u_low = split(u)
                p_high, p_low = scores[i]
                pu = dot(p_high, u_high) + (dot(p_low, u_high) + dot(p_high, u_low))
                read = (queries[i] - pu[:, 128:]).astype(BF)
                core = pu[:, :128] + dot(read, states_ref[pair, r])
                gate = gates[:, 128 * r:128 * r + 128]
                scale = lax.rsqrt(jnp.mean(core * core, axis=1, keepdims=True) + 1e-6)
                mixed_ref[t, r, pl.ds(s * LEN, LEN)] = (core * scale * gain * (gate * jax.nn.sigmoid(gate))).astype(BF)
                core_ref[pair, r, s] = core.astype(BF)
                read_ref[pair, r, s] = read
        mixed_copy(t).start()

    def partial(t):
        ours = mixed_ref[t, core_id]
        theirs = other_ref[t]
        for block in range(4):
            at = pl.ds(block * 512, 512)
            acc_ref[:, at] = dot(ours, weighted_ref[:, at], ((0,), (0,))) + dot(
                theirs, weighted_other_ref[:, at], ((0,), (0,))
            )

    def gradient_step(t):
        mixed_copy(t).wait()

        @pl.when(t == 0)
        def _():
            wt_copy.wait()

        partial(t)

        @pl.when(t < 6)
        def _():
            gsend_ref[t] = acc_ref[...].astype(BF)
            to_row(t).start()

        @pl.when(t == 6)
        def _():
            total = acc_ref[...]
            for slot in (0, 2, 4):
                to_row(slot).wait()
                total = total + grecv_ref[slot].astype(F32)
            gsend_ref[6] = total.astype(BF)
            to_column.start()

    def step(t, carry):
        forward_step(t)

        @pl.when(t == 0)
        def _():
            for copy in rw_copies:
                copy.wait()
            rewards = rewards_ref[...]
            count = GROUP * samples
            real = iota((GROUP, 8, 128), 1) < samples
            centre = jnp.sum(rewards, axis=(0, 1), keepdims=True) / count
            off = jnp.where(real, rewards - centre, 0.0)
            spread = jnp.sqrt(jnp.sum(off * off, axis=(0, 1), keepdims=True) / count)
            coefficient = ((reward_ref[...] - centre[0]) / jnp.maximum(spread[0], 0.6)) / LEN
            for s in range(samples):
                factor = coefficient[s:s + 1]
                for block in range(16):
                    at = pl.ds(block * 128, 128)
                    weighted_ref[pl.ds(s * LEN, LEN), at] = (cot_ref[s, :, at].astype(F32) * factor).astype(BF)
            wt_copy.start()

        @pl.when(t == 1)
        def _():
            own.wait()
            for copy in w1_copies:
                copy.wait()
            w2_copy.start()
            for copy in w3_copies:
                copy.start()
            w4_copies[0].start()

        @pl.when(t == 2)
        def _():
            w2_copy.wait()
            for copy in w3_far:
                copy.start()
            w4_copies[1].start()

        @pl.when(t == 6)
        def _():
            for o in range(3):
                w3_copies[o].wait()
                w4_copies[2 + o].start()

        @pl.when(t > 0)
        def _():
            gradient_step(t - 1)

        return carry

    lax.fori_loop(0, CHIPS, step, 0)
    for o in range(3):
        w3_far[o].wait()
        w4_copies[5 + o].start()
    mixed_copy(7).wait()
    partial(7)
    total = acc_ref[...]
    for slot in (1, 3, 5):
        to_row(slot).wait()
        total = total + grecv_ref[slot].astype(F32)
    to_column.wait()
    part_ref[...] = total + grecv_ref[6].astype(F32)
    for copy in w4_copies:
        copy.wait()


def first(q, k, v, g, small, gain, state, reward, cot, weight):
    samples, _, wide = v.shape
    heads = wide // 128
    pairs = heads // 2
    dma = pltpu.SemaphoreType.DMA
    vmem = pl.BlockSpec(memory_space=pltpu.VMEM)
    anywhere = pl.BlockSpec(memory_space=pl.ANY)
    tokens = samples * LEN
    return pl.pallas_call(
        functools.partial(first_kernel, samples),
        in_specs=[vmem] * 9 + [anywhere],
        out_specs=[vmem] * 4 + [anywhere],
        out_shape=[
            jax.ShapeDtypeStruct((pairs, 2, samples, LEN, 128), BF),
            jax.ShapeDtypeStruct((pairs, 2, samples, LEN, 128), BF),
            jax.ShapeDtypeStruct((tokens, wide), BF),
            jax.ShapeDtypeStruct((128, wide), F32),
            jax.ShapeDtypeStruct((GROUP, 2, wide // 2, wide // GROUP), BF),
        ],
        scratch_shapes=[
            pltpu.VMEM((10, LEN, LEN), BF),
            pltpu.VMEM((GROUP, 2, 128, 128), BF),
            pltpu.VMEM((GROUP, 8, 128), F32),
            pltpu.VMEM((pairs, 2, tokens, 128), BF),
            pltpu.VMEM((pairs, tokens, 128), BF),
            pltpu.VMEM((tokens, wide), BF),
            pltpu.VMEM((7, 128, wide), BF),
            pltpu.VMEM((7, 128, wide), BF),
            pltpu.VMEM((128, wide), F32),
            dma((7,)), dma((7,)), dma((7,)), dma((7,)), dma, dma, dma((8,)), dma((8,)), dma((7,)), dma((7,)),
            dma((7,)), dma((7,)), dma, dma, dma((6,)), dma((6,)), dma((8,)), dma((8,)), dma,
        ],
        compiler_params=pltpu.CompilerParams(
            collective_id=0, has_side_effects=True, vmem_limit_bytes=60 * 1024 * 1024
        ),
    )(q, k, v, g, small, gain, state, reward, cot, weight)


def second_kernel(
    samples, weighted_ref, g_ref, core_ref, read_ref, gain_ref, part_ref, all_ref,
    prefix_ref, grad_ref,
    pieces_ref, psend_ref, precv_ref, slices_ref, sum_ref,
    load_sem, p_send, p_recv, s_send, s_recv, a_send, a_recv,
):
    me = lax.axis_index("sample")

    def in_group(offset):
        return {"sample": lax.rem(me + offset, GROUP)}

    def load(u):
        pair = lax.rem(me + 1 + u, GROUP)
        return pltpu.make_async_copy(
            all_ref.at[:, :, lane_block(pair, 128)], pieces_ref.at[lax.rem(u, 2)], load_sem.at[lax.rem(u, 2)]
        )

    load(0).start()
    greet([in_group(o) for o in range(1, GROUP)])
    height = 128 // GROUP

    def slab(index):
        return pl.ds(pl.multiple_of(index * height, height), height)

    s_copies = [
        remote(part_ref.at[slab(lax.rem(me + o, GROUP))], slices_ref.at[o - 1], s_send.at[o - 1], s_recv.at[o - 1], in_group(o))
        for o in range(1, GROUP)
    ]
    for copy in s_copies:
        copy.start()
    a_copies = [
        remote(sum_ref, grad_ref.at[slab(me)], a_send.at[o - 1], a_recv.at[o - 1], in_group(o))
        for o in range(1, GROUP)
    ]
    gain = gain_ref[...]

    def prefix_copy(u):
        return remote(psend_ref.at[u], precv_ref.at[u], p_send.at[u], p_recv.at[u], in_group(u + 1))

    def pair_grads(u):
        pair = lax.rem(me + 1 + u, GROUP)
        load(u).wait()
        slot = lax.rem(u, 2)
        back = jnp.zeros((weighted_ref.shape[0], 256), F32)
        for block in range(GROUP):
            piece = pieces_ref[slot, block].reshape(256, 256)
            back = back + dot(weighted_ref[:, block * 256:block * 256 + 256], piece, ((1,), (1,)))
        grads = [jnp.zeros((128, 128), F32), jnp.zeros((128, 128), F32)]
        for s in range(samples):
            gates = g_ref[s, :, lane_block(pair, 256)].astype(F32)
            for r in range(2):
                core = core_ref[pair, r, s].astype(F32)
                gate = gates[:, 128 * r:128 * r + 128]
                scale = lax.rsqrt(jnp.mean(core * core, axis=1, keepdims=True) + 1e-6)
                normed = core * scale
                lifted = back[s * LEN:s * LEN + LEN, 128 * r:128 * r + 128] * gain * (gate * jax.nn.sigmoid(gate))
                core_grad = scale * (lifted - normed * jnp.mean(lifted * normed, axis=1, keepdims=True))
                grads[r] = grads[r] + dot(read_ref[pair, r, s], core_grad.astype(BF), ((0,), (0,)))
        return grads

    def step(u, carry):
        load(u + 1).start()
        grads = pair_grads(u)
        psend_ref[u, 0] = grads[0]
        psend_ref[u, 1] = grads[1]
        prefix_copy(u).start()

        @pl.when(u == 3)
        def _():
            total = part_ref[slab(me)]
            for o in range(GROUP - 1):
                s_copies[o].wait()
                total = total + slices_ref[o]
            sum_ref[...] = total
            grad_ref[slab(me)] = total
            for copy in a_copies:
                copy.start()

        return carry

    lax.fori_loop(0, GROUP - 1, step, 0)
    own = pair_grads(GROUP - 1)
    for u in range(GROUP - 1):
        prefix_copy(u).wait()
    for r in range(2):
        total = own[r]
        for u in range(GROUP - 1):
            total = total + precv_ref[u, r].astype(F32)
        prefix_ref[r] = total
    for copy in a_copies:
        copy.wait()


def second(weighted, g, core, read, gain, part, whole):
    samples, _, wide = g.shape
    dma = pltpu.SemaphoreType.DMA
    vmem = pl.BlockSpec(memory_space=pltpu.VMEM)
    return pl.pallas_call(
        functools.partial(second_kernel, samples),
        in_specs=[vmem] * 6 + [pl.BlockSpec(memory_space=pl.ANY)],
        out_specs=[vmem] * 2,
        out_shape=[
            jax.ShapeDtypeStruct((2, 128, 128), F32),
            jax.ShapeDtypeStruct((128, wide), F32),
        ],
        scratch_shapes=[
            pltpu.VMEM((2, GROUP, 2, 128, wide // GROUP), BF),
            pltpu.VMEM((7, 2, 128, 128), F32),
            pltpu.VMEM((7, 2, 128, 128), F32),
            pltpu.VMEM((7, 128 // GROUP, wide), F32),
            pltpu.VMEM((128 // GROUP, wide), F32),
            dma((2,)), dma((7,)), dma((7,)), dma((7,)), dma((7,)), dma((7,)), dma((7,)),
        ],
        compiler_params=pltpu.CompilerParams(
            collective_id=1, has_side_effects=True, vmem_limit_bytes=60 * 1024 * 1024
        ),
    )(weighted, g, core, read, gain, part, whole)


def adam_update(weight, first_moment, second_moment, gradient):
    first_new = 0.9 * first_moment + 0.1 * gradient
    second_new = 0.95 * second_moment + 0.05 * gradient * gradient
    direction = first_new / (1.0 - 0.9**10) / (jnp.sqrt(second_new / (1.0 - 0.95**10)) + 1e-08)
    weight_new = weight - 0.001 * (direction + 0.1 * weight)
    return (weight_new, first_new, second_new)


def local(
    query_vectors,
    key_vectors,
    value_vectors,
    output_gates,
    beta_logits,
    decay_logits,
    decay_rates,
    norm_gain,
    prefix_states,
    cotangent,
    rewards,
    out_weight,
    first_moment,
    second_moment,
):
    samples = rewards.shape[1]
    heads = beta_logits.shape[2]
    rows, wide = out_weight.shape
    weight16 = out_weight.astype(BF).reshape(rows, GROUP, wide // GROUP).transpose(1, 0, 2)
    decays = -decay_rates[:, None] * jax.nn.softplus(decay_logits[0].astype(F32))

    def by_pair(source):
        return source.reshape(samples, heads // 2, 2, LEN).transpose(1, 0, 2, 3).reshape(heads // 2, 2 * samples, LEN)

    small = jnp.concatenate([by_pair(beta_logits[0].astype(F32)), by_pair(decays)], axis=1)
    gain = norm_gain[None]
    gates = output_gates[0]
    reward_tile = jnp.broadcast_to(jnp.pad(rewards[0], (0, 8 - samples))[:, None], (8, 128))
    core, read, weighted, part, whole = first(
        query_vectors[0], key_vectors[0], value_vectors[0], gates, small, gain,
        prefix_states[0].astype(BF), reward_tile, cotangent[0], weight16,
    )
    prefix_grad, gradient = second(weighted, gates, core, read, gain, part, whole)
    return (prefix_grad[None],) + adam_update(out_weight, first_moment, second_moment, gradient)


def solution(mesh):
    placed = (
        P("dp", "sample", None, None),
        P("dp", "sample", None, None),
        P("dp", "sample", None, None),
        P("dp", "sample", None, None),
        P("dp", "sample", None, None),
        P("dp", "sample", None, None),
        P(),
        P(),
        P("dp", "sample", None, None),
        P("dp", "sample", None, None),
        P("dp", "sample"),
        P("dp", None),
        P("dp", None),
        P("dp", None),
    )
    return jax.shard_map(
        local,
        mesh=mesh,
        in_specs=placed,
        out_specs=(P("dp", "sample", None, None), P("dp", None), P("dp", None), P("dp", None)),
        check_vma=False,
    )
```

time: 446 us -> 163 us (0.37)
  waiting for transfers between devices: 236 us -> 0 us
  blocking collectives: 105 us -> 0 us
  Pallas kernels: 56 us -> 148 us
  matrix products: 17.6 us -> 0 us
  between operations: 15.9 us -> 0.74 us
    reduce_scatter x2 -> x0, waiting for transfers between devices: 166 us -> none  [the longest x1 93.2 us: local(): lax.psum_scatter(partial, 'dp', scatter_dimension=0, tiled=True)]
    pallas_call x2, Pallas kernels: 56 us -> 148 us  [the longest x1 101 us: first(): pl.pallas_call(functools.partial(first_kernel, samples), in_specs=[vmem]...]
    psum x1 -> x0, blocking collectives: 79.6 us -> none  [local(): gradient = lax.psum(partial_rows.astype(F32), 'sample')]
    all_gather x2 -> x0, waiting for transfers between devices: 68.7 us -> none  [the longest x1 51.4 us: local(): weight16 = lax.all_gather(out_weight.astype(BF), 'dp', axis=0, tiled=True)]
    unnamed x1 -> x0, blocking collectives: 25.7 us -> none
    dot_general x2 -> x0, matrix products: 17.6 us -> none  [the longest x1 10.7 us: local(): lax.dot_general(flat_weighted, weight16, (((1,), (1,)), ((), ())), prefer...]
  transfers between devices with their start and end apart: 4 -> 0, of which waited for: 4 -> 0; matrix products, arithmetic and copies ran while one was open for 1% -> 0% of each run, Pallas kernels for 0% -> 0%
where the time goes in v2:
time: 163 us; the launch traced here: 162 us
  Pallas kernels  148 us (91%)
  other arithmetic  6.43 us (4%)
  local copies, waits for them, and re-layouts  6.19 us (4%)
    pallas_call x1, Pallas kernels, first(): pl.pallas_call(functools.partial(first_kernel, samples), in_specs=[vmem]...  101 us
    pallas_call x1, Pallas kernels, second(): pl.pallas_call(functools.partial(second_kernel, samples), in_specs=[vmem]...  47.7 us
    sub x1, other arithmetic, adam_update(): weight_new = weight - 0.001 * (direction + 0.1 * weight)  3.51 us

profile of v2, /device:TPU:0, one launch (start us, length us, event | category | flops | bytes accessed | tf_op | source)
XLA Modules:
  0.0 161.8 jit_solution(1762683246937508622)
XLA Ops:
  0.6 0.7 neg.9
  1.3 0.7 pad.4
  1.9 0.7 broadcast_in_dim.7.reward_ref
  2.6 0.1 mul.44
  2.7 0.1 copy.38
  2.8 0.7 reshape.44
  3.6 0.7 copy.39
  4.3 0.1 fusion.1
  4.4 0.6 pad_maximum_fusion.small_ref
  5.0 1.5 convert_bitcast_fusion.state_ref
  6.6 1.5 copy.46
  8.1 1.0 copy.47
  9.1 100.8 %shard_map.165 = (bf16[8,2,2,256,128]{4,3,2,1,0:T(8,128)(2,1)}, bf16[8,2,2,256,128]{4,3,2,1,0:T(8,128)(2,1)}, bf16[512,2048]{1,0:T(8,128)(2,1)}, f32[128,2048]{1,0:T(8,128)}, bf16[8,2,1024,256]{3,2,1,0:T(8,128)(2,1)}) custom-call(bf16[2,256,1024]{2,1,0:T(8,128)(2,1)} %bitcast.27, bf16[2,256,1024]{2,1,0:T(8,128)(2,1)} %bitcast.28, ...), custom_call_target="tpu_custom_call" | custom-call | tf_op jit(solution)/shard_map/pallas_call | solution.py:341
  109.9 0.0 copy-start
  109.9 0.0 copy-start.1
  109.9 0.0 copy-start.2
  109.9 47.7 %shard_map.166 = (f32[2,128,128]{2,1,0:T(8,128)}, f32[128,2048]{1,0:T(8,128)}) custom-call(bf16[512,2048]{1,0:T(8,128)(2,1)} %get-tuple-element.11.weighted_ref, bf16[2,256,2048]{2,1,0:T(8,128)(2,1)} %bitcast.22, bf16[8,2,2,256,128]{4,3,2,1,0:T(8,128)(2,1)} %get-tuple-element.12.core_ref, bf16[8,2,2,256,128]{4,3,2,1,0:T(8,128)(2,1)} %get-tuple-element.13.read_ref, ...), custom_call_target="tpu_custom_call" | custom-call | tf_op jit(solution)/shard_map/pallas_call | solution.py:468
  157.6 0.0 copy-done
  157.6 0.0 copy-done.1
  157.6 0.0 copy-done.2
  157.6 0.0 copy-start.3
  157.6 3.5 %multiply_subtract_fusion = (f32[128,2048]{1,0:T(8,128)}, f32[128,2048]{1,0:T(8,128)}, f32[128,2048]{1,0:T(8,128)}) fusion(f32[128,2048]{1,0:T(8,128)S(1)} %copy-done, f32[128,2048]{1,0:T(8,128)} %get-tuple-element.17, f32[128,2048]{1,0:T(8,128)S(1)} %copy-done.1, f32[128,2048]{1,0:T(8,128)S(1)} %copy-done.2), kind=kLoop, calls=%fused_computation.2 | loop fusion | flops 3932160 | bytes 7340032 | tf_op jit(solution)/shard_map/sub | solution.py:494
  161.2 0.0 copy-done.3
  161.2 0.7 copy.53
  (3 shorter events, 0.1 us)
Async XLA Ops:
  109.9 47.7 %copy-start = (f32[128,2048]{1,0:T(8,128)S(1)}, f32[128,2048]{1,0:T(8,128)}, u32[]{:S(2)}) copy-start(f32[128,2048]{1,0:T(8,128)} %param.25) | copy-start | bytes 3145732
  109.9 47.7 %copy-start.1 = (f32[128,2048]{1,0:T(8,128)S(1)}, f32[128,2048]{1,0:T(8,128)}, u32[]{:S(2)}) copy-start(f32[128,2048]{1,0:T(8,128)} %param.26) | copy-start | bytes 3145732
  109.9 47.7 %copy-start.2 = (f32[128,2048]{1,0:T(8,128)S(1)}, f32[128,2048]{1,0:T(8,128)}, u32[]{:S(2)}) copy-start(f32[128,2048]{1,0:T(8,128)} %param.27) | copy-start | bytes 3145732
  157.6 3.5 %copy-start.3 = (f32[2,128,128]{2,1,0:T(8,128)S(1)}, f32[2,128,128]{2,1,0:T(8,128)}, u32[]{:S(2)}) copy-start(f32[2,128,128]{2,1,0:T(8,128)} %get-tuple-element.16) | copy-start | bytes 393220

commit v3 on v2

v3 whole, which is shorter than its diff:
```python
import functools
import jax
import jax.numpy as jnp
from jax import lax
from jax.experimental import pallas as pl
from jax.experimental.pallas import tpu as pltpu
from jax.sharding import PartitionSpec as P

LEN = 256
F32 = jnp.float32
BF = jnp.bfloat16
MESH = pl.DeviceIdType.MESH
CHIPS = 8
GROUP = 8


def dot(a, b, dims=((1,), (0,))):
    return lax.dot_general(a, b, (dims, ((), ())), preferred_element_type=F32)


def iota(shape, dim):
    return lax.broadcasted_iota(jnp.int32, shape, dim)


def split(x):
    high = x.astype(BF)
    return high, (x - high.astype(F32)).astype(BF)


def odd_rows(x, width):
    n = x.shape[0] // (2 * width)
    return x.reshape((n, 2, width) + x.shape[1:])[:, 1].reshape((n * width,) + x.shape[1:])


def put_odd(x, rows, width):
    n = x.shape[0] // (2 * width)
    parted = x.reshape((n, 2, width) + x.shape[1:])
    rows = rows.reshape((n, width) + x.shape[1:])
    return jnp.stack([parted[:, 0], parted[:, 1] - rows], axis=1).reshape(x.shape)


def inverses(systems, masks_ref):
    count = len(systems)
    eye = masks_ref[8]
    results = [eye - a * masks_ref[0] for a in systems]
    for level in range(1, 8):
        width = 1 << level
        mask = masks_ref[level]
        if width < 16:
            lefts = [dot(results[i], systems[i] * mask).astype(BF) for i in range(count)]
            fixes = [dot(lefts[i], results[i]).astype(BF) for i in range(count)]
            results = [results[i] - fixes[i] for i in range(count)]
        else:
            lefts = [dot(odd_rows(results[i], width), systems[i] * mask).astype(BF) for i in range(count)]
            fixes = [dot(lefts[i], results[i]).astype(BF) for i in range(count)]
            results = [put_odd(results[i], fixes[i], width) for i in range(count)]
    return [r - eye for r in results]


def places():
    dp = lax.axis_index("dp")
    return lax.div(dp, 4), lax.rem(lax.div(dp, 2), 2), lax.rem(dp, 2), lax.axis_index("sample")


def remote(src, dst, send, recv, where):
    return pltpu.make_async_remote_copy(
        src_ref=src, dst_ref=dst, send_sem=send, recv_sem=recv, device_id=where, device_id_type=MESH
    )


def lane_block(index, width):
    return pl.ds(pl.multiple_of(index * width, width), width)


def whole_kernel(
    samples, rate_ref, reward_ref, gain_ref, beta_ref, decay_ref, state_ref, weight_ref,
    q_in, k_in, v_in, g_in, cot_in,
    prefix_ref, grad_ref,
    q_ref, k_ref, v_ref, g_ref, cot_ref,
    masks_ref, small_ref, states_ref, rewards_ref, tile_ref, mixed_ref, other_ref, weighted_ref, weighted_other_ref,
    core_ref, read_ref, all_ref, gsend_ref, grecv_ref, acc_ref, part_ref, slices_ref, sum_ref, psend_ref, precv_ref,
    in_sem, st_send, st_recv, rw_send, rw_recv, wt_send, wt_recv, mx_send, mx_recv, g_send, g_recv,
    w1_send, w1_recv, w2_send, w2_recv, w3_send, w3_recv, w4_send, w4_recv,
    s_send, s_recv, a_send, a_recv, p_send, p_recv,
):
    loads = [
        pltpu.make_async_copy(source, target, in_sem.at[i])
        for i, (source, target) in enumerate(
            ((k_in, k_ref), (q_in, q_ref), (v_in, v_ref), (g_in, g_ref), (cot_in, cot_ref))
        )
    ]
    for copy in loads:
        copy.start()
    x, yl, core_id, me = places()
    chip = x * 2 + yl
    y_hi, z = lax.div(me, 4), lax.rem(me, 4)
    far = (1 - y_hi) * 4 + z
    sibling = {"dp": chip * 2 + 1 - core_id, "sample": me}
    column = {"dp": (x * 2 + 1 - yl) * 2 + core_id, "sample": me}

    def at_chip(index):
        return {"dp": index * 2 + core_id, "sample": me}

    def in_group(offset):
        return {"sample": lax.rem(me + offset, GROUP)}

    def along_z(offset):
        return y_hi * 4 + lax.rem(z + offset, 4)

    def far_along_z(offset):
        return (1 - y_hi) * 4 + lax.rem(z + offset, 4)

    chip_peers = [lax.rem(x + t // 2, 4) * 2 + lax.rem(yl + t % 2, 2) for t in range(1, CHIPS)]
    group_peers = [in_group(o) for o in range(1, GROUP)]
    others = [sibling] + [at_chip(c) for c in chip_peers] + group_peers
    barrier = pltpu.get_barrier_semaphore()
    for partner in others:
        pl.semaphore_signal(barrier, inc=1, device_id=partner, device_id_type=MESH)

    states_ref[me] = state_ref[...].astype(BF)
    mine = all_ref.at[me, core_id, lane_block(chip, 128)]
    mine[...] = weight_ref[:, lane_block(me, 256)].astype(BF)
    tile_row = iota((8, 128), 0)
    tile = jnp.zeros((8, 128), F32)
    for s in range(samples):
        tile = jnp.where(tile_row == s, reward_ref[0, s], tile)
    tile_ref[...] = tile
    rewards_ref[me] = tile
    for s in range(samples):
        betas = beta_ref[s].astype(F32)
        softs = jax.nn.softplus(decay_ref[s].astype(F32))
        for pair in range(betas.shape[0] // 2):
            small_ref[pair, 2 * s:2 * s + 2] = betas[2 * pair:2 * pair + 2]
            small_ref[pair, 2 * (samples + s):2 * (samples + s) + 2] = softs[2 * pair:2 * pair + 2]
    rows = iota((LEN, LEN), 0)
    cols = iota((LEN, LEN), 1)
    for level in range(8):
        same = (rows >> (level + 1)) == (cols >> (level + 1))
        below = (rows >> level) > (cols >> level)
        masks_ref[level] = jnp.where(same & below, 1.0, 0.0).astype(BF)
    masks_ref[8] = jnp.where(rows == cols, 1.0, 0.0).astype(BF)
    masks_ref[9] = jnp.where(rows <= cols, 1.0, 0.0).astype(BF)
    gain = gain_ref[...]
    pl.semaphore_wait(barrier, len(others))

    st_copies = [
        remote(states_ref.at[me], states_ref.at[me], st_send.at[o], st_recv.at[o], group_peers[o])
        for o in range(GROUP - 1)
    ]
    rw_copies = [
        remote(tile_ref, rewards_ref.at[me], rw_send.at[o], rw_recv.at[o], group_peers[o]) for o in range(GROUP - 1)
    ]
    w1_copies = [
        remote(mine, mine, w1_send.at[t], w1_recv.at[t], at_chip(chip_peers[t])) for t in range(CHIPS - 1)
    ]
    for copy in st_copies + rw_copies + w1_copies:
        copy.start()

    held = all_ref.at[me, core_id]
    far_held = all_ref.at[far, core_id]
    w2_copy = remote(held, held, w2_send, w2_recv, {"sample": far})
    w3_near = [
        remote(held, held, w3_send.at[i], w3_recv.at[i], {"sample": along_z(o)}) for i, o in ((0, 1), (1, 3))
    ]
    w3_far = [
        remote(far_held, far_held, w3_send.at[i], w3_recv.at[i], {"sample": along_z(o)}) for i, o in ((2, 1), (3, 3))
    ]

    def passed(index, half, slot, offset):
        piece = all_ref.at[index, core_id, pl.ds(half * 512, 512)]
        return remote(piece, piece, w3_send.at[slot], w3_recv.at[slot], {"sample": along_z(offset)})

    w3_near_on = [passed(along_z(3), 0, 4, 1), passed(along_z(1), 1, 5, 3)]
    w3_far_on = [passed(far_along_z(3), 0, 6, 1), passed(far_along_z(1), 1, 7, 3)]

    def shared(index, slot):
        piece = all_ref.at[index, core_id]
        return remote(piece, piece, w4_send.at[slot], w4_recv.at[slot], sibling)

    w4_copies = [shared(me, 0), shared(far, 1)]
    w4_copies += [shared(along_z(1), 2), shared(along_z(3), 3), shared(far_along_z(1), 4), shared(far_along_z(3), 5)]
    w4_copies += [shared(along_z(2), 6), shared(far_along_z(2), 7)]

    def shift_at(t):
        u = lax.div(t, 2)
        return 2 - u + 3 * lax.div(u, 2) - 2 * lax.div(u, 3)

    def pair_at(t):
        return lax.rem(x + shift_at(t), 4) * 2 + lax.rem(yl + 1 - lax.rem(t, 2), 2)

    wt_copy = remote(weighted_ref, weighted_other_ref, wt_send, wt_recv, sibling)

    def mixed_copy(t):
        return remote(mixed_ref.at[t, 1 - core_id], other_ref.at[t], mx_send.at[t], mx_recv.at[t], sibling)

    def to_row(t):
        target = lax.rem(x + shift_at(t), 4) * 2 + yl
        return remote(gsend_ref.at[t], grecv_ref.at[t], g_send.at[t], g_recv.at[t], at_chip(target))

    def to_column(t):
        return remote(gsend_ref.at[t], grecv_ref.at[t], g_send.at[t], g_recv.at[t], column)

    def forward_step(t):
        pair = pair_at(t)
        raw = small_ref[pair]
        raw_row = iota(raw.shape, 0)
        rate = jnp.where(lax.rem(raw_row, 2) == 0, rate_ref[2 * pair], rate_ref[2 * pair + 1])
        small = raw * -rate
        first = small.astype(BF)
        rest = small - first.astype(F32)
        second = rest.astype(BF)
        third = (rest - second.astype(F32)).astype(BF)
        upper = masks_ref[9]
        running = dot(first, upper) + dot(second, upper) + dot(third, upper)
        by_row = jnp.where(raw_row < 2 * samples, jax.nn.sigmoid(raw), running)
        columns = by_row.T
        causal = rows >= cols
        strict = rows > cols
        diagonal = rows == cols
        systems, scores, rights, queries = [], [], [], []
        for s in range(samples):
            q = q_ref[s, :, lane_block(pair, 128)]
            k = k_ref[s, :, lane_block(pair, 128)]
            qk = dot(jnp.concatenate([k, q], axis=0), k, ((1,), (1,)))
            kk, qk = qk[:LEN], qk[LEN:]
            kf = k.astype(F32)
            qf = q.astype(F32)
            k_row = lax.rsqrt(jnp.sum(jnp.where(diagonal, kk, 0.0), axis=0, keepdims=True) + 1e-6)
            k_col = lax.rsqrt(jnp.sum(kf * kf, axis=1, keepdims=True) + 1e-6)
            q_col = lax.rsqrt(jnp.sum(qf * qf, axis=1, keepdims=True) + 1e-6) * (128 ** -0.5)
            kk = kk * k_row
            qk = qk * k_row
            v = v_ref[s, :, lane_block(pair, 256)].astype(F32)
            for r in range(2):
                i = 2 * s + r
                beta = columns[:, i:i + 1]
                c_col = columns[:, 2 * samples + i:2 * samples + i + 1]
                c_row = by_row[2 * samples + i:2 * samples + i + 1]
                falloff = jnp.exp(jnp.where(causal, c_col - c_row, 0.0))
                a = jnp.where(strict, falloff * kk * (beta * k_col), 0.0)
                p = jnp.where(causal, falloff * qk * q_col, 0.0)
                growth = jnp.exp(c_col)
                systems.append(a.astype(BF))
                scores.append(split(p))
                rights.append(
                    jnp.concatenate([beta * v[:, 128 * r:128 * r + 128], (beta * growth * k_col) * kf], axis=1)
                )
                queries.append((growth * q_col) * qf)
        solved = inverses(systems, masks_ref)

        @pl.when(t == 0)
        def _():
            for copy in st_copies:
                copy.wait()

        for s in range(samples):
            gates = g_ref[s, :, lane_block(pair, 256)].astype(F32)
            for r in range(2):
                i = 2 * s + r
                u = rights[i] + dot(solved[i], rights[i].astype(BF))
                u_high, u_low = split(u)
                p_high, p_low = scores[i]
                pu = dot(p_high, u_high) + (dot(p_low, u_high) + dot(p_high, u_low))
                read = (queries[i] - pu[:, 128:]).astype(BF)
                core = pu[:, :128] + dot(read, states_ref[pair, r])
                gate = gates[:, 128 * r:128 * r + 128]
                scale = lax.rsqrt(jnp.mean(core * core, axis=1, keepdims=True) + 1e-6)
                mixed_ref[t, r, pl.ds(s * LEN, LEN)] = (core * scale * gain * (gate * jax.nn.sigmoid(gate))).astype(BF)
                core_ref[pair, r, s] = core.astype(BF)
                read_ref[pair, r, s] = read
        mixed_copy(t).start()

    def weigh():
        for copy in rw_copies:
            copy.wait()
        rewards = rewards_ref[...]
        count = GROUP * samples
        real = iota((GROUP, 8, 128), 1) < samples
        centre = jnp.sum(rewards, axis=(0, 1), keepdims=True) / count
        off = jnp.where(real, rewards - centre, 0.0)
        spread = jnp.sqrt(jnp.sum(off * off, axis=(0, 1), keepdims=True) / count)
        coefficient = ((tile_ref[...] - centre[0]) / jnp.maximum(spread[0], 0.6)) / LEN
        for s in range(samples):
            factor = coefficient[s:s + 1]
            for block in range(16):
                at = pl.ds(block * 128, 128)
                weighted_ref[pl.ds(s * LEN, LEN), at] = (cot_ref[s, :, at].astype(F32) * factor).astype(BF)
        wt_copy.start()

    def partial(t):
        ours = mixed_ref[t, core_id]
        theirs = other_ref[t]
        for block in range(4):
            at = pl.ds(block * 512, 512)
            acc_ref[:, at] = dot(ours, weighted_ref[:, at], ((0,), (0,))) + dot(
                theirs, weighted_other_ref[:, at], ((0,), (0,))
            )

    def gradient_step(t):
        mixed_copy(t).wait()

        @pl.when(t == 0)
        def _():
            wt_copy.wait()

        partial(t)

        @pl.when(t == 0)
        def _():
            gsend_ref[0] = acc_ref[...].astype(BF)
            to_column(0).start()

        @pl.when(t == 1)
        def _():
            to_column(0).wait()
            gsend_ref[1] = (acc_ref[...] + grecv_ref[0].astype(F32)).astype(BF)
            to_row(1).start()

        @pl.when((t > 1) & (t < 6))
        def _():
            gsend_ref[t] = acc_ref[...].astype(BF)
            to_row(t).start()

        @pl.when(t == 6)
        def _():
            total = acc_ref[...]
            for slot in (2, 4):
                to_row(slot).wait()
                total = total + grecv_ref[slot].astype(F32)
            gsend_ref[6] = total.astype(BF)
            to_column(6).start()

    for copy in loads:
        copy.wait()

    def step(t, carry):
        forward_step(t)

        @pl.when(t == 0)
        def _():
            weigh()

        @pl.when(t == 1)
        def _():
            for copy in w1_copies:
                copy.wait()
            w2_copy.start()
            for copy in w3_near:
                copy.start()
            w4_copies[0].start()

        @pl.when(t == 2)
        def _():
            w2_copy.wait()
            for copy in w3_far:
                copy.start()
            w4_copies[1].start()

        @pl.when(t == 3)
        def _():
            for copy in w3_near:
                copy.wait()
            for copy in w3_near_on:
                copy.start()
            w4_copies[2].start()
            w4_copies[3].start()

        @pl.when(t == 5)
        def _():
            for copy in w3_far:
                copy.wait()
            for copy in w3_far_on:
                copy.start()
            w4_copies[4].start()
            w4_copies[5].start()

        @pl.when(t == 6)
        def _():
            for copy in w3_near_on:
                copy.wait()
            w4_copies[6].start()

        @pl.when(t > 0)
        def _():
            gradient_step(t - 1)

        return carry

    lax.fori_loop(0, CHIPS, step, 0)
    for copy in w3_far_on:
        copy.wait()
    w4_copies[7].start()
    mixed_copy(7).wait()
    partial(7)
    total = acc_ref[...]
    for slot in (1, 3, 5):
        to_row(slot).wait()
        total = total + grecv_ref[slot].astype(F32)
    to_column(6).wait()
    total = total + grecv_ref[6].astype(F32)
    acc_ref[...] = total
    part_ref[...] = total.astype(BF)

    height = 128 // GROUP

    def slab(index):
        return pl.ds(pl.multiple_of(index * height, height), height)

    s_copies = [
        remote(
            part_ref.at[slab(lax.rem(me + o, GROUP))], slices_ref.at[o - 1], s_send.at[o - 1], s_recv.at[o - 1], in_group(o)
        )
        for o in range(1, GROUP)
    ]
    for copy in s_copies:
        copy.start()
    a_copies = [
        remote(sum_ref, grad_ref.at[slab(me)], a_send.at[o - 1], a_recv.at[o - 1], in_group(o))
        for o in range(1, GROUP)
    ]
    for copy in w4_copies:
        copy.wait()

    def prefix_copy(u):
        return remote(psend_ref.at[u], precv_ref.at[u], p_send.at[u], p_recv.at[u], in_group(u + 1))

    def pair_grads(u):
        pair = lax.rem(me + 1 + u, GROUP)
        back = jnp.zeros((weighted_ref.shape[0], 256), F32)
        for block in range(GROUP):
            piece = all_ref[block, :, lane_block(pair, 128)].reshape(256, 256)
            back = back + dot(weighted_ref[:, block * 256:block * 256 + 256], piece, ((1,), (1,)))
        grads = [jnp.zeros((128, 128), F32), jnp.zeros((128, 128), F32)]
        for s in range(samples):
            gates = g_ref[s, :, lane_block(pair, 256)].astype(F32)
            for r in range(2):
                core = core_ref[pair, r, s].astype(F32)
                gate = gates[:, 128 * r:128 * r + 128]
                scale = lax.rsqrt(jnp.mean(core * core, axis=1, keepdims=True) + 1e-6)
                normed = core * scale
                lifted = back[s * LEN:s * LEN + LEN, 128 * r:128 * r + 128] * gain * (gate * jax.nn.sigmoid(gate))
                core_grad = scale * (lifted - normed * jnp.mean(lifted * normed, axis=1, keepdims=True))
                high, low = split(core_grad)
                read = read_ref[pair, r, s]
                grads[r] = grads[r] + dot(read, high, ((0,), (0,))) + dot(read, low, ((0,), (0,)))
        return grads

    def back_step(u, carry):
        grads = pair_grads(u)
        psend_ref[u, 0] = grads[0].astype(BF)
        psend_ref[u, 1] = grads[1].astype(BF)
        prefix_copy(u).start()

        @pl.when(u == 2)
        def _():
            total = acc_ref[slab(me)]
            for o in range(GROUP - 1):
                s_copies[o].wait()
                total = total + slices_ref[o].astype(F32)
            sum_ref[...] = total
            grad_ref[slab(me)] = total
            for copy in a_copies:
                copy.start()

        return carry

    lax.fori_loop(0, GROUP - 1, back_step, 0)
    own = pair_grads(GROUP - 1)
    for u in range(GROUP - 1):
        prefix_copy(u).wait()
    for r in range(2):
        total = own[r]
        for u in range(GROUP - 1):
            total = total + precv_ref[u, r].astype(F32)
        prefix_ref[r] = total
    for copy in a_copies:
        copy.wait()


def whole(rates, rewards, gain, beta, decay, state, weight, q, k, v, g, cot):
    samples, _, wide = v.shape
    pairs = wide // 256
    tokens = samples * LEN
    dma = pltpu.SemaphoreType.DMA
    vmem = pl.BlockSpec(memory_space=pltpu.VMEM)
    smem = pl.BlockSpec(memory_space=pltpu.SMEM)
    anywhere = pl.BlockSpec(memory_space=pl.ANY)
    sems = [dma((5,))]
    for count in (7, 7, None, 8, 7, 7, None, 8, 8, 7, 7, 7):
        sems += [dma if count is None else dma((count,))] * 2
    return pl.pallas_call(
        functools.partial(whole_kernel, samples),
        in_specs=[smem, smem] + [vmem] * 5 + [anywhere] * 5,
        out_specs=[vmem] * 2,
        out_shape=[
            jax.ShapeDtypeStruct((2, 128, 128), F32),
            jax.ShapeDtypeStruct((128, wide), F32),
        ],
        scratch_shapes=[
            pltpu.VMEM(q.shape, BF),
            pltpu.VMEM(k.shape, BF),
            pltpu.VMEM(v.shape, BF),
            pltpu.VMEM(g.shape, BF),
            pltpu.VMEM(cot.shape, BF),
            pltpu.VMEM((10, LEN, LEN), BF),
            pltpu.VMEM((pairs, 4 * samples, LEN), F32),
            pltpu.VMEM((GROUP, 2, 128, 128), BF),
            pltpu.VMEM((GROUP, 8, 128), F32),
            pltpu.VMEM((8, 128), F32),
            pltpu.VMEM((pairs, 2, tokens, 128), BF),
            pltpu.VMEM((pairs, tokens, 128), BF),
            pltpu.VMEM((tokens, wide), BF),
            pltpu.VMEM((tokens, wide), BF),
            pltpu.VMEM((pairs, 2, samples, LEN, 128), BF),
            pltpu.VMEM((pairs, 2, samples, LEN, 128), BF),
            pltpu.VMEM((GROUP, 2, wide // 2, wide // GROUP), BF),
            pltpu.VMEM((7, 128, wide), BF),
            pltpu.VMEM((7, 128, wide), BF),
            pltpu.VMEM((128, wide), F32),
            pltpu.VMEM((128, wide), BF),
            pltpu.VMEM((7, 128 // GROUP, wide), BF),
            pltpu.VMEM((128 // GROUP, wide), F32),
            pltpu.VMEM((7, 2, 128, 128), BF),
            pltpu.VMEM((7, 2, 128, 128), BF),
        ] + sems,
        compiler_params=pltpu.CompilerParams(
            collective_id=0, has_side_effects=True, vmem_limit_bytes=62 * 1024 * 1024
        ),
    )(rates, rewards, gain, beta, decay, state, weight, q, k, v, g, cot)


def adam_update(weight, first_moment, second_moment, gradient):
    first_new = 0.9 * first_moment + 0.1 * gradient
    second_new = 0.95 * second_moment + 0.05 * gradient * gradient
    direction = first_new / (1.0 - 0.9**10) / (jnp.sqrt(second_new / (1.0 - 0.95**10)) + 1e-08)
    weight_new = weight - 0.001 * (direction + 0.1 * weight)
    return (weight_new, first_new, second_new)


def local(
    query_vectors,
    key_vectors,
    value_vectors,
    output_gates,
    beta_logits,
    decay_logits,
    decay_rates,
    norm_gain,
    prefix_states,
    cotangent,
    rewards,
    out_weight,
    first_moment,
    second_moment,
):
    prefix_grad, gradient = whole(
        decay_rates, rewards, norm_gain[None], beta_logits[0], decay_logits[0], prefix_states[0], out_weight,
        query_vectors[0], key_vectors[0], value_vectors[0], output_gates[0], cotangent[0],
    )
    return (prefix_grad[None],) + adam_update(out_weight, first_moment, second_moment, gradient)


def solution(mesh):
    placed = (
        P("dp", "sample", None, None),
        P("dp", "sample", None, None),
        P("dp", "sample", None, None),
        P("dp", "sample", None, None),
        P("dp", "sample", None, None),
        P("dp", "sample", None, None),
        P(),
        P(),
        P("dp", "sample", None, None),
        P("dp", "sample", None, None),
        P("dp", "sample"),
        P("dp", None),
        P("dp", None),
        P("dp", None),
    )
    return jax.shard_map(
        local,
        mesh=mesh,
        in_specs=placed,
        out_specs=(P("dp", "sample", None, None), P("dp", None), P("dp", None), P("dp", None)),
        check_vma=False,
    )
```

time: 163 us -> 128 us (0.79)
  Pallas kernels: 148 us -> 121 us
  local copies, waits for them, and re-layouts: 6.19 us -> 0.66 us
  other arithmetic: 6.43 us -> 4.14 us
    pallas_call x2 -> x1, Pallas kernels: 148 us -> 121 us  [whole(): pl.pallas_call(functools.partial(whole_kernel, samples), in_specs=[smem,...]
    reshape x5 -> x0, local copies, waits for them, and re-layouts: 1.81 us -> none  [the longest x1 1.01 us: local(): out_weight.astype(BF).reshape(rows, GROUP, wide // GROUP).transpose(1, 0, 2)]
where the time goes in v3:
time: 128 us; the launch traced here: 127 us
  Pallas kernels  121 us (95%)
  other arithmetic  4.14 us (3%)
    pallas_call x1, Pallas kernels, whole(): pl.pallas_call(functools.partial(whole_kernel, samples), in_specs=[smem,...  121 us
    sub x1, other arithmetic, adam_update(): weight_new = weight - 0.001 * (direction + 0.1 * weight)  4.14 us

profile of v3, /device:TPU:0, one launch (start us, length us, event | category | flops | bytes accessed | tf_op | source)
XLA Modules:
  0.0 126.9 jit_solution(4724199674273207574)
XLA Ops:
  0.6 0.0 copy-start
  0.6 121.5 %shard_map.165 = (f32[2,128,128]{2,1,0:T(8,128)}, f32[128,2048]{1,0:T(8,128)}) custom-call(f32[16]{0:T(128)} %rate_ref.1, f32[1,2]{1,0:T(1,128)} %reward_ref.1, f32[1,128]{1,0:T(1,128)} %bitcast.19, bf16[2,16,256]{2,1,0:T(8,128)(2,1)} %bitcast.17, bf16[2,16,256]{2,1,0:T(8,128)(2,1)} %bitcast.18, f32[2,128,128]{2,1,0:T(8,128)} %bitcast.15, ...), custom_call_target="tpu_custom_call" | custom-call | tf_op jit(solution)/shard_map/pallas_call | solution.py:491
  122.1 0.0 copy-done
  122.1 0.0 copy-start.1
  122.1 4.1 %multiply_subtract_fusion = (f32[128,2048]{1,0:T(8,128)}, f32[128,2048]{1,0:T(8,128)}, f32[128,2048]{1,0:T(8,128)}) fusion(f32[128,2048]{1,0:T(8,128)S(1)} %copy-done, f32[128,2048]{1,0:T(8,128)} %get-tuple-element.7, f32[128,2048]{1,0:T(8,128)} %param.26, f32[128,2048]{1,0:T(8,128)} %param.27), kind=kLoop, calls=%fused_computation.2 | loop fusion | flops 3932160 | bytes 7340032 | tf_op jit(solution)/shard_map/sub | solution.py:536
  126.3 0.0 copy-done.1
  126.3 0.7 copy.19
Async XLA Ops:
  0.6 121.5 %copy-start = (f32[128,2048]{1,0:T(8,128)S(1)}, f32[128,2048]{1,0:T(8,128)}, u32[]{:S(2)}) copy-start(f32[128,2048]{1,0:T(8,128)} %weight_ref.1) | copy-start | bytes 3145732
  122.1 4.2 %copy-start.1 = (f32[2,128,128]{2,1,0:T(8,128)S(1)}, f32[2,128,128]{2,1,0:T(8,128)}, u32[]{:S(2)}) copy-start(f32[2,128,128]{2,1,0:T(8,128)} %get-tuple-element.6) | copy-start | bytes 393220

commit v4 on v3

--- a/solution.py
+++ b/solution.py
@@ -7,6 +7,7 @@
 from jax.sharding import PartitionSpec as P
 
 LEN = 256
+HALF = 128
 F32 = jnp.float32
 BF = jnp.bfloat16
 MESH = pl.DeviceIdType.MESH
@@ -41,9 +42,9 @@
 
 def inverses(systems, masks_ref):
     count = len(systems)
-    eye = masks_ref[8]
+    eye = masks_ref[7]
     results = [eye - a * masks_ref[0] for a in systems]
-    for level in range(1, 8):
+    for level in range(1, 7):
         width = 1 << level
         mask = masks_ref[level]
         if width < 16:
@@ -77,7 +78,7 @@
     q_in, k_in, v_in, g_in, cot_in,
     prefix_ref, grad_ref,
     q_ref, k_ref, v_ref, g_ref, cot_ref,
-    masks_ref, small_ref, states_ref, rewards_ref, tile_ref, mixed_ref, other_ref, weighted_ref, weighted_other_ref,
+    masks_ref, upper_ref, small_ref, states_ref, rewards_ref, tile_ref, mixed_ref, other_ref, weighted_ref, weighted_other_ref,
     core_ref, read_ref, all_ref, gsend_ref, grecv_ref, acc_ref, part_ref, slices_ref, sum_ref, psend_ref, precv_ref,
     in_sem, st_send, st_recv, rw_send, rw_recv, wt_send, wt_recv, mx_send, mx_recv, g_send, g_recv,
     w1_send, w1_recv, w2_send, w2_recv, w3_send, w3_recv, w4_send, w4_recv,
@@ -132,14 +133,14 @@
         for pair in range(betas.shape[0] // 2):
             small_ref[pair, 2 * s:2 * s + 2] = betas[2 * pair:2 * pair + 2]
             small_ref[pair, 2 * (samples + s):2 * (samples + s) + 2] = softs[2 * pair:2 * pair + 2]
-    rows = iota((LEN, LEN), 0)
-    cols = iota((LEN, LEN), 1)
-    for level in range(8):
+    upper_ref[...] = jnp.where(iota((LEN, LEN), 0) <= iota((LEN, LEN), 1), 1.0, 0.0).astype(BF)
+    rows = iota((HALF, HALF), 0)
+    cols = iota((HALF, HALF), 1)
+    for level in range(7):
         same = (rows >> (level + 1)) == (cols >> (level + 1))
         below = (rows >> level) > (cols >> level)
         masks_ref[level] = jnp.where(same & below, 1.0, 0.0).astype(BF)
-    masks_ref[8] = jnp.where(rows == cols, 1.0, 0.0).astype(BF)
-    masks_ref[9] = jnp.where(rows <= cols, 1.0, 0.0).astype(BF)
+    masks_ref[7] = jnp.where(rows == cols, 1.0, 0.0).astype(BF)
     gain = gain_ref[...]
     pl.semaphore_wait(barrier, len(others))
 
@@ -153,7 +154,7 @@
     w1_copies = [
         remote(mine, mine, w1_send.at[t], w1_recv.at[t], at_chip(chip_peers[t])) for t in range(CHIPS - 1)
     ]
-    for copy in st_copies + rw_copies + w1_copies:
+    for copy in rw_copies + st_copies + w1_copies:
         copy.start()
 
     held = all_ref.at[me, core_id]
@@ -182,11 +183,12 @@
     w4_copies += [shared(along_z(2), 6), shared(far_along_z(2), 7)]
 
     def shift_at(t):
-        u = lax.div(t, 2)
-        return 2 - u + 3 * lax.div(u, 2) - 2 * lax.div(u, 3)
+        m = lax.rem(t, 3)
+        return (2 - m + 3 * lax.div(m, 2)) * (1 - lax.div(t, 6))
 
     def pair_at(t):
-        return lax.rem(x + shift_at(t), 4) * 2 + lax.rem(yl + 1 - lax.rem(t, 2), 2)
+        turn = 1 - lax.rem(lax.div(t, 3), 2) - lax.div(t, 7)
+        return lax.rem(x + shift_at(t), 4) * 2 + lax.rem(yl + turn, 2)
 
     wt_copy = remote(weighted_ref, weighted_other_ref, wt_send, wt_recv, sibling)
 
@@ -210,40 +212,48 @@
         rest = small - first.astype(F32)
         second = rest.astype(BF)
         third = (rest - second.astype(F32)).astype(BF)
-        upper = masks_ref[9]
+        upper = upper_ref[...]
         running = dot(first, upper) + dot(second, upper) + dot(third, upper)
         by_row = jnp.where(raw_row < 2 * samples, jax.nn.sigmoid(raw), running)
         columns = by_row.T
         causal = rows >= cols
         strict = rows > cols
         diagonal = rows == cols
-        systems, scores, rights, queries = [], [], [], []
+        systems, belows, scores, rights, queries = [], [], [], [], []
         for s in range(samples):
             q = q_ref[s, :, lane_block(pair, 128)]
             k = k_ref[s, :, lane_block(pair, 128)]
-            qk = dot(jnp.concatenate([k, q], axis=0), k, ((1,), (1,)))
-            kk, qk = qk[:LEN], qk[LEN:]
+            top = dot(jnp.concatenate([k[:HALF], q[:HALF]], axis=0), k[:HALF], ((1,), (1,)))
+            low = dot(jnp.concatenate([k[HALF:], q[HALF:]], axis=0), k, ((1,), (1,)))
             kf = k.astype(F32)
             qf = q.astype(F32)
-            k_row = lax.rsqrt(jnp.sum(jnp.where(diagonal, kk, 0.0), axis=0, keepdims=True) + 1e-6)
+            row_first = lax.rsqrt(jnp.sum(jnp.where(diagonal, top[:HALF], 0.0), axis=0, keepdims=True) + 1e-6)
+            row_second = lax.rsqrt(jnp.sum(jnp.where(diagonal, low[:HALF, HALF:], 0.0), axis=0, keepdims=True) + 1e-6)
             k_col = lax.rsqrt(jnp.sum(kf * kf, axis=1, keepdims=True) + 1e-6)
             q_col = lax.rsqrt(jnp.sum(qf * qf, axis=1, keepdims=True) + 1e-6) * (128 ** -0.5)
-            kk = kk * k_row
-            qk = qk * k_row
+            top = top * row_first
+            low_first = low[:, :HALF] * row_first
+            low_second = low[:, HALF:] * row_second
             v = v_ref[s, :, lane_block(pair, 256)].astype(F32)
             for r in range(2):
                 i = 2 * s + r
                 beta = columns[:, i:i + 1]
                 c_col = columns[:, 2 * samples + i:2 * samples + i + 1]
                 c_row = by_row[2 * samples + i:2 * samples + i + 1]
-                falloff = jnp.exp(jnp.where(causal, c_col - c_row, 0.0))
-                a = jnp.where(strict, falloff * kk * (beta * k_col), 0.0)
-                p = jnp.where(causal, falloff * qk * q_col, 0.0)
+                beta_k = beta * k_col
+                f_top = jnp.exp(jnp.where(causal, c_col[:HALF] - c_row[:, :HALF], 0.0))
+                f_low = jnp.exp(c_col[HALF:] - c_row[:, :HALF])
+                f_end = jnp.exp(jnp.where(causal, c_col[HALF:] - c_row[:, HALF:], 0.0))
+                systems.append(jnp.where(strict, f_top * top[:HALF] * beta_k[:HALF], 0.0).astype(BF))
+                systems.append(jnp.where(strict, f_end * low_second[:HALF] * beta_k[HALF:], 0.0).astype(BF))
+                belows.append((f_low * low_first[:HALF] * beta_k[HALF:]).astype(BF))
+                p_top = jnp.where(causal, f_top * top[HALF:] * q_col[:HALF], 0.0)
+                p_low = f_low * low_first[HALF:] * q_col[HALF:]
+                p_end = jnp.where(causal, f_end * low_second[HALF:] * q_col[HALF:], 0.0)
+                scores.append((split(p_top), split(jnp.concatenate([p_low, p_end], axis=1))))
                 growth = jnp.exp(c_col)
-                systems.append(a.astype(BF))
-                scores.append(split(p))
                 rights.append(
-                    jnp.concatenate([beta * v[:, 128 * r:128 * r + 128], (beta * growth * k_col) * kf], axis=1)
+                    jnp.concatenate([beta * v[:, 128 * r:128 * r + 128], (growth * beta_k) * kf], axis=1)
                 )
                 queries.append((growth * q_col) * qf)
         solved = inverses(systems, masks_ref)
@@ -257,10 +267,17 @@
             gates = g_ref[s, :, lane_block(pair, 256)].astype(F32)
             for r in range(2):
                 i = 2 * s + r
-                u = rights[i] + dot(solved[i], rights[i].astype(BF))
-                u_high, u_low = split(u)
-                p_high, p_low = scores[i]
-                pu = dot(p_high, u_high) + (dot(p_low, u_high) + dot(p_high, u_low))
+                right = rights[i][:HALF]
+                first_high, first_low = split(right + dot(solved[2 * i], right.astype(BF)))
+                right = rights[i][HALF:] - dot(belows[i], first_high)
+                second_high, second_low = split(right + dot(solved[2 * i + 1], right.astype(BF)))
+                u_high = jnp.concatenate([first_high, second_high], axis=0)
+                u_low = jnp.concatenate([first_low, second_low], axis=0)
+                (top_high, top_low), (low_high, low_low) = scores[i]
+                pu = jnp.concatenate([
+                    dot(top_high, first_high) + (dot(top_low, first_high) + dot(top_high, first_low)),
+                    dot(low_high, u_high) + (dot(low_low, u_high) + dot(low_high, u_low)),
+                ], axis=0)
                 read = (queries[i] - pu[:, 128:]).astype(BF)
                 core = pu[:, :128] + dot(read, states_ref[pair, r])
                 gate = gates[:, 128 * r:128 * r + 128]
@@ -305,18 +322,7 @@
 
         partial(t)
 
-        @pl.when(t == 0)
-        def _():
-            gsend_ref[0] = acc_ref[...].astype(BF)
-            to_column(0).start()
-
-        @pl.when(t == 1)
-        def _():
-            to_column(0).wait()
-            gsend_ref[1] = (acc_ref[...] + grecv_ref[0].astype(F32)).astype(BF)
-            to_row(1).start()
-
-        @pl.when((t > 1) & (t < 6))
+        @pl.when(t < 6)
         def _():
             gsend_ref[t] = acc_ref[...].astype(BF)
             to_row(t).start()
@@ -324,7 +330,7 @@
         @pl.when(t == 6)
         def _():
             total = acc_ref[...]
-            for slot in (2, 4):
+            for slot in (0, 1, 2):
                 to_row(slot).wait()
                 total = total + grecv_ref[slot].astype(F32)
             gsend_ref[6] = total.astype(BF)
@@ -332,74 +338,68 @@
 
     for copy in loads:
         copy.wait()
+    weigh()
+
+    def weights_on(t, begin):
+        if begin:
+            @pl.when(t == 1)
+            def _():
+                for copy in w1_copies:
+                    copy.wait()
+                w2_copy.start()
+                for copy in w3_near:
+                    copy.start()
+                w4_copies[0].start()
+
+            @pl.when(t == 3)
+            def _():
+                w2_copy.wait()
+                for copy in w3_far:
+                    copy.start()
+                w4_copies[1].start()
+
+            @pl.when(t == 4)
+            def _():
+                for copy in w3_near:
+                    copy.wait()
+                for copy in w3_near_on:
+                    copy.start()
+                w4_copies[2].start()
+                w4_copies[3].start()
+
+            @pl.when(t == 6)
+            def _():
+                for copy in w3_near_on:
+                    copy.wait()
+                w4_copies[6].start()
+        else:
+            @pl.when(t == 5)
+            def _():
+                for copy in w3_far:
+                    copy.wait()
+                for copy in w3_far_on:
+                    copy.start()
+                w4_copies[4].start()
+                w4_copies[5].start()
 
     def step(t, carry):
         forward_step(t)
 
-        @pl.when(t == 0)
-        def _():
-            weigh()
-
-        @pl.when(t == 1)
-        def _():
-            for copy in w1_copies:
-                copy.wait()
-            w2_copy.start()
-            for copy in w3_near:
-                copy.start()
-            w4_copies[0].start()
-
-        @pl.when(t == 2)
-        def _():
-            w2_copy.wait()
-            for copy in w3_far:
-                copy.start()
-            w4_copies[1].start()
-
-        @pl.when(t == 3)
-        def _():
-            for copy in w3_near:
-                copy.wait()
-            for copy in w3_near_on:
-                copy.start()
-            w4_copies[2].start()
-            w4_copies[3].start()
-
-        @pl.when(t == 5)
-        def _():
-            for copy in w3_far:
-                copy.wait()
-            for copy in w3_far_on:
-                copy.start()
-            w4_copies[4].start()
-            w4_copies[5].start()
-
-        @pl.when(t == 6)
-        def _():
-            for copy in w3_near_on:
-                copy.wait()
-            w4_copies[6].start()
+        weights_on(t, True)
 
         @pl.when(t > 0)
         def _():
             gradient_step(t - 1)
 
+        weights_on(t, False)
         return carry
 
     lax.fori_loop(0, CHIPS, step, 0)
+    mixed_copy(7).wait()
+    partial(7)
     for copy in w3_far_on:
         copy.wait()
     w4_copies[7].start()
-    mixed_copy(7).wait()
-    partial(7)
-    total = acc_ref[...]
-    for slot in (1, 3, 5):
-        to_row(slot).wait()
-        total = total + grecv_ref[slot].astype(F32)
-    to_column(6).wait()
-    total = total + grecv_ref[6].astype(F32)
-    acc_ref[...] = total
-    part_ref[...] = total.astype(BF)
 
     height = 128 // GROUP
 
@@ -412,8 +412,6 @@
         )
         for o in range(1, GROUP)
     ]
-    for copy in s_copies:
-        copy.start()
     a_copies = [
         remote(sum_ref, grad_ref.at[slab(me)], a_send.at[o - 1], a_recv.at[o - 1], in_group(o))
         for o in range(1, GROUP)
@@ -452,6 +450,19 @@
         prefix_copy(u).start()
 
         @pl.when(u == 2)
+        def _():
+            total = acc_ref[...]
+            for slot in (3, 4, 5):
+                to_row(slot).wait()
+                total = total + grecv_ref[slot].astype(F32)
+            to_column(6).wait()
+            total = total + grecv_ref[6].astype(F32)
+            acc_ref[...] = total
+            part_ref[...] = total.astype(BF)
+            for copy in s_copies:
+                copy.start()
+
+        @pl.when(u == 5)
         def _():
             total = acc_ref[slab(me)]
             for o in range(GROUP - 1):
@@ -502,7 +513,8 @@
             pltpu.VMEM(v.shape, BF),
             pltpu.VMEM(g.shape, BF),
             pltpu.VMEM(cot.shape, BF),
-            pltpu.VMEM((10, LEN, LEN), BF),
+            pltpu.VMEM((8, HALF, HALF), BF),
+            pltpu.VMEM((LEN, LEN), BF),
             pltpu.VMEM((pairs, 4 * samples, LEN), F32),
             pltpu.VMEM((GROUP, 2, 128, 128), BF),
             pltpu.VMEM((GROUP, 8, 128), F32),

time: 128 us -> 111 us (0.87)
  Pallas kernels: 121 us -> 104 us
    pallas_call x1, Pallas kernels: 121 us -> 104 us  [whole(): pl.pallas_call(functools.partial(whole_kernel, samples), in_specs=[smem,...]
where the time goes in v4:
time: 111 us; the launch traced here: 109 us
  Pallas kernels  104 us (94%)
  other arithmetic  4.14 us (4%)
    pallas_call x1, Pallas kernels, whole(): pl.pallas_call(functools.partial(whole_kernel, samples), in_specs=[smem,...  104 us
    sub x1, other arithmetic, adam_update(): weight_new = weight - 0.001 * (direction + 0.1 * weight)  4.14 us

profile of v4, /device:TPU:0, one launch (start us, length us, event | category | flops | bytes accessed | tf_op | source)
XLA Modules:
  0.0 109.2 jit_solution(2801828167916415928)
XLA Ops:
  0.6 0.0 copy-start
  0.6 103.8 %shard_map.165 = (f32[2,128,128]{2,1,0:T(8,128)}, f32[128,2048]{1,0:T(8,128)}) custom-call(f32[16]{0:T(128)} %rate_ref.1, f32[1,2]{1,0:T(1,128)} %reward_ref.1, f32[1,128]{1,0:T(1,128)} %bitcast.19, bf16[2,16,256]{2,1,0:T(8,128)(2,1)} %bitcast.17, bf16[2,16,256]{2,1,0:T(8,128)(2,1)} %bitcast.18, f32[2,128,128]{2,1,0:T(8,128)} %bitcast.15, ...), custom_call_target="tpu_custom_call" | custom-call | tf_op jit(solution)/shard_map/pallas_call | solution.py:502
  104.4 0.0 copy-done
  104.4 0.0 copy-start.1
  104.4 4.1 %multiply_subtract_fusion = (f32[128,2048]{1,0:T(8,128)}, f32[128,2048]{1,0:T(8,128)}, f32[128,2048]{1,0:T(8,128)}) fusion(f32[128,2048]{1,0:T(8,128)S(1)} %copy-done, f32[128,2048]{1,0:T(8,128)} %get-tuple-element.7, f32[128,2048]{1,0:T(8,128)} %param.26, f32[128,2048]{1,0:T(8,128)} %param.27), kind=kLoop, calls=%fused_computation.2 | loop fusion | flops 3932160 | bytes 7340032 | tf_op jit(solution)/shard_map/sub | solution.py:548
  108.6 0.0 copy-done.1
  108.6 0.7 copy.19
Async XLA Ops:
  0.6 103.8 %copy-start = (f32[128,2048]{1,0:T(8,128)S(1)}, f32[128,2048]{1,0:T(8,128)}, u32[]{:S(2)}) copy-start(f32[128,2048]{1,0:T(8,128)} %weight_ref.1) | copy-start | bytes 3145732
  104.4 4.2 %copy-start.1 = (f32[2,128,128]{2,1,0:T(8,128)S(1)}, f32[2,128,128]{2,1,0:T(8,128)}, u32[]{:S(2)}) copy-start(f32[2,128,128]{2,1,0:T(8,128)} %get-tuple-element.6) | copy-start | bytes 393220

commit v5 on v4

--- a/solution.py
+++ b/solution.py
@@ -258,10 +258,15 @@
                 queries.append((growth * q_col) * qf)
         solved = inverses(systems, masks_ref)
 
-        @pl.when(t == 0)
-        def _():
+        if isinstance(t, int):
             for copy in st_copies:
                 copy.wait()
+            for copy in w1_copies:
+                copy.wait()
+            w2_copy.start()
+            for copy in w3_near:
+                copy.start()
+            w4_copies[0].start()
 
         for s in range(samples):
             gates = g_ref[s, :, lane_block(pair, 256)].astype(F32)
@@ -305,13 +310,10 @@
         wt_copy.start()
 
     def partial(t):
-        ours = mixed_ref[t, core_id]
-        theirs = other_ref[t]
+        both = jnp.concatenate([mixed_ref[t, core_id], other_ref[t]], axis=0).T
         for block in range(4):
             at = pl.ds(block * 512, 512)
-            acc_ref[:, at] = dot(ours, weighted_ref[:, at], ((0,), (0,))) + dot(
-                theirs, weighted_other_ref[:, at], ((0,), (0,))
-            )
+            acc_ref[:, at] = dot(both, jnp.concatenate([weighted_ref[:, at], weighted_other_ref[:, at]], axis=0))
 
     def gradient_step(t):
         mixed_copy(t).wait()
@@ -322,7 +324,18 @@
 
         partial(t)
 
-        @pl.when(t < 6)
+        @pl.when(t == 0)
+        def _():
+            gsend_ref[0] = acc_ref[...].astype(BF)
+            to_column(0).start()
+
+        @pl.when(t == 3)
+        def _():
+            to_column(0).wait()
+            gsend_ref[3] = (acc_ref[...] + grecv_ref[0].astype(F32)).astype(BF)
+            to_row(3).start()
+
+        @pl.when((t > 0) & (t < 6) & (t != 3))
         def _():
             gsend_ref[t] = acc_ref[...].astype(BF)
             to_row(t).start()
@@ -330,7 +343,7 @@
         @pl.when(t == 6)
         def _():
             total = acc_ref[...]
-            for slot in (0, 1, 2):
+            for slot in (1, 2):
                 to_row(slot).wait()
                 total = total + grecv_ref[slot].astype(F32)
             gsend_ref[6] = total.astype(BF)
@@ -340,61 +353,46 @@
         copy.wait()
     weigh()
 
-    def weights_on(t, begin):
-        if begin:
-            @pl.when(t == 1)
-            def _():
-                for copy in w1_copies:
-                    copy.wait()
-                w2_copy.start()
-                for copy in w3_near:
-                    copy.start()
-                w4_copies[0].start()
-
-            @pl.when(t == 3)
-            def _():
-                w2_copy.wait()
-                for copy in w3_far:
-                    copy.start()
-                w4_copies[1].start()
-
-            @pl.when(t == 4)
-            def _():
-                for copy in w3_near:
-                    copy.wait()
-                for copy in w3_near_on:
-                    copy.start()
-                w4_copies[2].start()
-                w4_copies[3].start()
-
-            @pl.when(t == 6)
-            def _():
-                for copy in w3_near_on:
-                    copy.wait()
-                w4_copies[6].start()
-        else:
-            @pl.when(t == 5)
-            def _():
-                for copy in w3_far:
-                    copy.wait()
-                for copy in w3_far_on:
-                    copy.start()
-                w4_copies[4].start()
-                w4_copies[5].start()
-
     def step(t, carry):
         forward_step(t)
 
-        weights_on(t, True)
-
-        @pl.when(t > 0)
-        def _():
-            gradient_step(t - 1)
-
-        weights_on(t, False)
+        gradient_step(t - 1)
+
+        @pl.when(t == 3)
+        def _():
+            for copy in w3_near:
+                copy.wait()
+            for copy in w3_near_on:
+                copy.start()
+            w4_copies[2].start()
+            w4_copies[3].start()
+
+        @pl.when(t == 5)
+        def _():
+            for copy in w3_near_on:
+                copy.wait()
+            w4_copies[6].start()
+
+        @pl.when(t == 2)
+        def _():
+            w2_copy.wait()
+            for copy in w3_far:
+                copy.start()
+            w4_copies[1].start()
+
+        @pl.when(t == 4)
+        def _():
+            for copy in w3_far:
+                copy.wait()
+            for copy in w3_far_on:
+                copy.start()
+            w4_copies[4].start()
+            w4_copies[5].start()
+
         return carry
 
-    lax.fori_loop(0, CHIPS, step, 0)
+    forward_step(0)
+    lax.fori_loop(1, CHIPS, step, 0)
     mixed_copy(7).wait()
     partial(7)
     for copy in w3_far_on:
@@ -424,10 +422,8 @@
 
     def pair_grads(u):
         pair = lax.rem(me + 1 + u, GROUP)
-        back = jnp.zeros((weighted_ref.shape[0], 256), F32)
-        for block in range(GROUP):
-            piece = all_ref[block, :, lane_block(pair, 128)].reshape(256, 256)
-            back = back + dot(weighted_ref[:, block * 256:block * 256 + 256], piece, ((1,), (1,)))
+        pieces = [all_ref[block, :, lane_block(pair, 128)].reshape(256, 256) for block in range(GROUP)]
+        back = dot(weighted_ref[...], jnp.concatenate(pieces, axis=1), ((1,), (1,)))
         grads = [jnp.zeros((128, 128), F32), jnp.zeros((128, 128), F32)]
         for s in range(samples):
             gates = g_ref[s, :, lane_block(pair, 256)].astype(F32)
@@ -449,7 +445,7 @@
         psend_ref[u, 1] = grads[1].astype(BF)
         prefix_copy(u).start()
 
-        @pl.when(u == 2)
+        @pl.when(u == 3)
         def _():
             total = acc_ref[...]
             for slot in (3, 4, 5):
@@ -462,7 +458,7 @@
             for copy in s_copies:
                 copy.start()
 
-        @pl.when(u == 5)
+        @pl.when(u == 6)
         def _():
             total = acc_ref[slab(me)]
             for o in range(GROUP - 1):

time: 111 us -> 110 us (level); the launches traced: 109 us -> 110 us
  no operation moved by 1% of the time
where the time goes in v5:
time: 110 us
  Pallas kernels  104 us (95%)
  other arithmetic  4.14 us (4%)
    pallas_call x1, Pallas kernels, whole(): pl.pallas_call(functools.partial(whole_kernel, samples), in_specs=[smem,...  104 us
    sub x1, other arithmetic, adam_update(): weight_new = weight - 0.001 * (direction + 0.1 * weight)  4.14 us

profile of v5, /device:TPU:0, one launch (start us, length us, event | category | flops | bytes accessed | tf_op | source)
XLA Modules:
  0.0 109.8 jit_solution(12816066549479310201)
XLA Ops:
  0.6 0.0 copy-start
  0.6 104.3 %shard_map.165 = (f32[2,128,128]{2,1,0:T(8,128)}, f32[128,2048]{1,0:T(8,128)}) custom-call(f32[16]{0:T(128)} %rate_ref.1, f32[1,2]{1,0:T(1,128)} %reward_ref.1, f32[1,128]{1,0:T(1,128)} %bitcast.19, bf16[2,16,256]{2,1,0:T(8,128)(2,1)} %bitcast.17, bf16[2,16,256]{2,1,0:T(8,128)(2,1)} %bitcast.18, f32[2,128,128]{2,1,0:T(8,128)} %bitcast.15, ...), custom_call_target="tpu_custom_call" | custom-call | tf_op jit(solution)/shard_map/pallas_call | solution.py:498
  105.0 0.0 copy-done
  105.0 0.0 copy-start.1
  105.0 4.1 %multiply_subtract_fusion = (f32[128,2048]{1,0:T(8,128)}, f32[128,2048]{1,0:T(8,128)}, f32[128,2048]{1,0:T(8,128)}) fusion(f32[128,2048]{1,0:T(8,128)S(1)} %copy-done, f32[128,2048]{1,0:T(8,128)} %get-tuple-element.7, f32[128,2048]{1,0:T(8,128)} %param.26, f32[128,2048]{1,0:T(8,128)} %param.27), kind=kLoop, calls=%fused_computation.2 | loop fusion | flops 3932160 | bytes 7340032 | tf_op jit(solution)/shard_map/sub | solution.py:544
  109.1 0.0 copy-done.1
  109.1 0.7 copy.19
Async XLA Ops:
  0.6 104.3 %copy-start = (f32[128,2048]{1,0:T(8,128)S(1)}, f32[128,2048]{1,0:T(8,128)}, u32[]{:S(2)}) copy-start(f32[128,2048]{1,0:T(8,128)} %weight_ref.1) | copy-start | bytes 3145732
  105.0 4.2 %copy-start.1 = (f32[2,128,128]{2,1,0:T(8,128)S(1)}, f32[2,128,128]{2,1,0:T(8,128)}, u32[]{:S(2)}) copy-start(f32[2,128,128]{2,1,0:T(8,128)} %get-tuple-element.6) | copy-start | bytes 393220
